TPU v7x, 32 devices: a whole 2x2x4 slice. The times are simulated.
32 devices in a mesh: dp: 2 (over core), ctx: 8 (over z, y), fsdp: 2 (over x).
Axes of the slice: x: 2, y: 2, z: 4, core: 2. Of those that a mesh axis runs over, the one named last changes fastest.
Arguments:
- tokens: bfloat16 [4, 2048, 1024], P(('dp', 'fsdp'), 'ctx'), may hold values from -6 to 6
- segment_ids: int32 [4, 2048], P(('dp', 'fsdp'), 'ctx'), may hold values from 0 to 15, never falling along the last dimension, each value on 1 to 1280 neighbouring positions
- w_query: bfloat16 [1024, 1024], P(('ctx', 'fsdp')), may hold values from -0.1875 to 0.1875
- b_query: bfloat16 [1024], P(('ctx', 'fsdp')), may hold values from -3 to 3
- w_key: bfloat16 [1024, 1024], P(('ctx', 'fsdp')), may hold values from -0.1875 to 0.1875
- w_value: bfloat16 [1024, 1024], P(('ctx', 'fsdp')), may hold values from -0.1875 to 0.1875
- b_value: bfloat16 [1024], P(('ctx', 'fsdp')), may hold values from -3 to 3
- w_out: bfloat16 [1024, 1024], P(('ctx', 'fsdp')), may hold values from -1.5 to 1.5
- b_out: bfloat16 [1024], P(('ctx', 'fsdp')), may hold values from -3 to 3
- g_attn: bfloat16 [1024], P(('ctx', 'fsdp')), may hold values from 0.5 to 1.5
- n_attn: bfloat16 [1024], P(('ctx', 'fsdp')), may hold values from -3 to 3
- w_in: bfloat16 [1024, 4096], P(('ctx', 'fsdp')), may hold values from -0.1875 to 0.1875
- b_in: bfloat16 [4096], P(('ctx', 'fsdp')), may hold values from -3 to 3
- w_back: bfloat16 [4096, 1024], P(('ctx', 'fsdp')), may hold values from -0.09375 to 0.09375
- b_back: bfloat16 [1024], P(('ctx', 'fsdp')), may hold values from -3 to 3
- g_ffn: bfloat16 [1024], P(('ctx', 'fsdp')), may hold values from 0.5 to 1.5
- n_ffn: bfloat16 [1024], P(('ctx', 'fsdp')), may hold values from -3 to 3
- cotangent: bfloat16 [4, 2048, 1024], P(('dp', 'fsdp'), 'ctx'), may hold values from -6 to 6
Outputs:
- output: bfloat16 [4, 2048, 1024], P(('dp', 'fsdp'), 'ctx')
- grad_tokens: float32 [4, 2048, 1024], P(('dp', 'fsdp'), 'ctx')
- grad_w_query: float32 [1024, 1024], P(('ctx', 'fsdp'))
- grad_b_query: float32 [1024], P(('ctx', 'fsdp'))
- grad_w_key: float32 [1024, 1024], P(('ctx', 'fsdp'))
- grad_w_value: float32 [1024, 1024], P(('ctx', 'fsdp'))
- grad_b_value: float32 [1024], P(('ctx', 'fsdp'))
- grad_w_out: float32 [1024, 1024], P(('ctx', 'fsdp'))
- grad_b_out: float32 [1024], P(('ctx', 'fsdp'))
- grad_g_attn: float32 [1024], P(('ctx', 'fsdp'))
- grad_n_attn: float32 [1024], P(('ctx', 'fsdp'))
- grad_w_in: float32 [1024, 4096], P(('ctx', 'fsdp'))
- grad_b_in: float32 [4096], P(('ctx', 'fsdp'))
- grad_w_back: float32 [4096, 1024], P(('ctx', 'fsdp'))
- grad_b_back: float32 [1024], P(('ctx', 'fsdp'))
- grad_g_ffn: float32 [1024], P(('ctx', 'fsdp'))
- grad_n_ffn: float32 [1024], P(('ctx', 'fsdp'))
Inputs may be any that keep to these rules, and one draw needn't show every extreme that they name: `segment_ids`: along a sequence the ids never fall; each of the 16 ids names 1 to 1280 consecutive tokens, and some document has exactly 1280 tokens.
All inputs are finite; a program needn't handle non-finite values.
Results may differ from a plain program's by a relative error of at most 0.017.
Values may be sent and summed in bfloat16 or wider, within the bound.
No kernel may reach another device: no remote copies, remote signals or barrier semaphores. Data moves between devices by JAX's collectives and lax.ppermute only.
A program may use at most 192 MiB of HBM per device.

v0:
```python
from functools import partial
import math

import jax
import jax.numpy as jnp
from jax import lax
from jax.sharding import PartitionSpec as P

D = 1024
H = 16
HD = 64


NORM_EPS = 1e-05
NEG_FILL = -1e30


def layer_norm_forward(hidden, norm_gain, norm_shift):
    centered_input = hidden - jnp.mean(hidden, -1, keepdims=True)
    inverse_deviation = lax.rsqrt(
        jnp.mean(centered_input * centered_input, -1, keepdims=True) + NORM_EPS
    )
    standardized_input = centered_input * inverse_deviation
    return (standardized_input * norm_gain + norm_shift, standardized_input, inverse_deviation)


def layer_norm_backward(upstream_gradient, standardized_input, inverse_deviation, norm_gain):
    scaled_rows = upstream_gradient * norm_gain
    centered_input = (
        scaled_rows
        - jnp.mean(scaled_rows, -1, keepdims=True)
        - standardized_input * jnp.mean(scaled_rows * standardized_input, -1, keepdims=True)
    )
    return (
        inverse_deviation * centered_input,
        jnp.sum(upstream_gradient * standardized_input, 0),
        jnp.sum(upstream_gradient, 0),
    )


def split_heads(columns):
    return columns.reshape(columns.shape[0], -1, HD)


def columns_of(matrix, col_start, col_width):
    return lax.dynamic_slice_in_dim(matrix, col_start, col_width, 1)


def group_logits(query_cols, key_cols, same_doc):
    scores = jnp.einsum(
        "thd,khd->htk",
        split_heads(query_cols),
        split_heads(key_cols),
        preferred_element_type=jnp.float32,
    ) * (1.0 / math.sqrt(HD))
    return jnp.where(same_doc[None], scores, NEG_FILL)


def contract_rows(left, right):
    return jnp.einsum("td,te->de", left, right, preferred_element_type=jnp.float32)


def times_transposed(left, matrix):
    return jnp.einsum("te,fe->tf", left, matrix, preferred_element_type=jnp.float32)


def attend_forward(query_rows, key_rows, value_rows, same_doc):
    row_count = query_rows.shape[0]
    group_heads = min(2, H)
    col_width = group_heads * HD

    def group_step(block_no, buffers):
        out_buf, total_buf = buffers
        col_start = block_no * col_width
        logits = group_logits(
            columns_of(query_rows, col_start, col_width),
            columns_of(key_rows, col_start, col_width),
            same_doc,
        )
        row_max = jnp.max(logits, -1, keepdims=True)
        exp_block = jnp.exp(logits - row_max)
        row_sum = jnp.sum(exp_block, -1, keepdims=True)
        probs_low = (exp_block / row_sum).astype(jnp.bfloat16)
        heads_out = jnp.einsum(
            "htk,khd->thd",
            probs_low,
            split_heads(columns_of(value_rows, col_start, col_width)),
            preferred_element_type=jnp.float32,
        )
        out_buf = lax.dynamic_update_slice_in_dim(
            out_buf, heads_out.reshape(row_count, col_width), col_start, 1
        )
        total_buf = lax.dynamic_update_slice_in_dim(
            total_buf, (row_max + jnp.log(row_sum))[:, :, 0], block_no * group_heads, 0
        )
        return (out_buf, total_buf)

    initial = (jnp.zeros((row_count, D), jnp.float32), jnp.zeros((H, row_count), jnp.float32))
    return lax.fori_loop(0, D // col_width, group_step, initial)


def attend_backward(query_rows, key_rows, value_rows, grad_rows, total_rows, same_doc):
    query_count = query_rows.shape[0]
    key_count = key_rows.shape[0]
    group_heads = min(2, H)
    col_width = group_heads * HD
    score_scale = 1.0 / math.sqrt(HD)

    def group_step(block_no, buffers):
        query_buf, delta_buf, key_buf, value_buf = buffers
        col_start = block_no * col_width
        head_start = block_no * group_heads
        query_cols = columns_of(query_rows, col_start, col_width)
        key_cols = columns_of(key_rows, col_start, col_width)
        value_cols = columns_of(value_rows, col_start, col_width)
        grad_cols = columns_of(grad_rows, col_start, col_width)
        log_total = lax.dynamic_slice_in_dim(total_rows, head_start, group_heads, 0)
        probs = jnp.exp(group_logits(query_cols, key_cols, same_doc) - log_total[:, :, None])
        grad_prob = jnp.einsum(
            "thd,khd->htk",
            split_heads(grad_cols),
            split_heads(value_cols),
            preferred_element_type=jnp.float32,
        )
        row_delta = jnp.sum(probs * grad_prob, -1)
        grad_score = (probs * (grad_prob - row_delta[:, :, None])).astype(jnp.bfloat16)
        grad_query = (
            jnp.einsum(
                "htk,khd->thd",
                grad_score,
                split_heads(key_cols),
                preferred_element_type=jnp.float32,
            )
            * score_scale
        )
        query_buf = lax.dynamic_update_slice_in_dim(
            query_buf, grad_query.reshape(query_count, col_width), col_start, 1
        )
        delta_buf = lax.dynamic_update_slice_in_dim(delta_buf, row_delta, head_start, 0)
        grad_key = (
            jnp.einsum(
                "htk,thd->khd",
                grad_score,
                split_heads(query_cols),
                preferred_element_type=jnp.float32,
            )
            * score_scale
        )
        grad_value = jnp.einsum(
            "htk,thd->khd",
            probs.astype(jnp.bfloat16),
            split_heads(grad_cols),
            preferred_element_type=jnp.float32,
        )
        key_buf = lax.dynamic_update_slice_in_dim(
            key_buf, grad_key.reshape(key_count, col_width), col_start, 1
        )
        value_buf = lax.dynamic_update_slice_in_dim(
            value_buf, grad_value.reshape(key_count, col_width), col_start, 1
        )
        return (query_buf, delta_buf, key_buf, value_buf)

    query_init = (
        jnp.zeros((query_count, D), jnp.float32),
        jnp.zeros((H, query_count), jnp.float32),
    )
    key_init = (jnp.zeros((key_count, D), jnp.float32), jnp.zeros((key_count, D), jnp.float32))
    return lax.fori_loop(0, D // col_width, group_step, query_init + key_init)


def body(
    tokens,
    segment_ids,
    w_query,
    b_query,
    w_key,
    w_value,
    b_value,
    w_out,
    b_out,
    g_attn,
    n_attn,
    w_in,
    b_in,
    w_back,
    b_back,
    g_ffn,
    n_ffn,
    cotangent,
):
    shards = (
        w_query,
        b_query,
        w_key,
        w_value,
        b_value,
        w_out,
        b_out,
        g_attn,
        n_attn,
        w_in,
        b_in,
        w_back,
        b_back,
        g_ffn,
        n_ffn,
    )
    gathered = (
        lax.all_gather(shards[0], ("ctx", "fsdp"), axis=0, tiled=True),
        lax.all_gather(shards[1], ("ctx", "fsdp"), axis=0, tiled=True),
        lax.all_gather(shards[2], ("ctx", "fsdp"), axis=0, tiled=True),
        lax.all_gather(shards[3], ("ctx", "fsdp"), axis=0, tiled=True),
        lax.all_gather(shards[4], ("ctx", "fsdp"), axis=0, tiled=True),
        lax.all_gather(shards[5], ("ctx", "fsdp"), axis=0, tiled=True),
        lax.all_gather(shards[6], ("ctx", "fsdp"), axis=0, tiled=True),
        lax.all_gather(shards[7], ("ctx", "fsdp"), axis=0, tiled=True),
        lax.all_gather(shards[8], ("ctx", "fsdp"), axis=0, tiled=True),
        lax.all_gather(shards[9], ("ctx", "fsdp"), axis=0, tiled=True),
        lax.all_gather(shards[10], ("ctx", "fsdp"), axis=0, tiled=True),
        lax.all_gather(shards[11], ("ctx", "fsdp"), axis=0, tiled=True),
        lax.all_gather(shards[12], ("ctx", "fsdp"), axis=0, tiled=True),
        lax.all_gather(shards[13], ("ctx", "fsdp"), axis=0, tiled=True),
        lax.all_gather(shards[14], ("ctx", "fsdp"), axis=0, tiled=True),
    )
    (
        query_mat,
        query_bias,
        key_mat,
        value_mat,
        value_bias,
        out_mat,
        out_bias,
        attention_norm_gain,
        attn_shift,
        in_mat,
        in_bias,
        back_mat,
        back_bias,
        feedforward_norm_gain,
        feedforward_norm_shift,
    ) = gathered
    inputs = tokens[0]
    doc_marks = segment_ids[0].astype(jnp.bfloat16)
    query_rows = (
        jnp.dot(inputs, query_mat, preferred_element_type=jnp.float32) + query_bias
    ).astype(jnp.bfloat16)
    key_rows = jnp.dot(inputs, key_mat, preferred_element_type=jnp.float32).astype(jnp.bfloat16)
    value_rows = (
        jnp.dot(inputs, value_mat, preferred_element_type=jnp.float32) + value_bias
    ).astype(jnp.bfloat16)
    all_keys, all_values, all_marks = (
        lax.all_gather(key_rows, "ctx", axis=0, tiled=True),
        lax.all_gather(value_rows, "ctx", axis=0, tiled=True),
        lax.all_gather(doc_marks, "ctx", axis=0, tiled=True),
    )
    same_doc = doc_marks[:, None] == all_marks[None, :]
    attended, log_total = attend_forward(query_rows, all_keys, all_values, same_doc)
    attended = attended.astype(jnp.bfloat16)
    branch = jnp.dot(attended, out_mat, preferred_element_type=jnp.float32) + out_bias
    normalized_rows, standardized_one, inverse_deviation_one = layer_norm_forward(
        inputs.astype(jnp.float32) + branch, attention_norm_gain, attn_shift
    )
    normed_low = normalized_rows.astype(jnp.bfloat16)
    inner = jnp.dot(normed_low, in_mat, preferred_element_type=jnp.float32) + in_bias
    active, gelu_pullback = jax.vjp(partial(jax.nn.gelu, approximate=False), inner)
    active_low = active.astype(jnp.bfloat16)
    feedforward_output = (
        jnp.dot(active_low, back_mat, preferred_element_type=jnp.float32) + back_bias
    )
    norm_result, standardized_two, inverse_deviation_two = layer_norm_forward(
        normalized_rows + feedforward_output, feedforward_norm_gain, feedforward_norm_shift
    )
    output_gradient = cotangent[0].astype(jnp.float32)
    grad_sum_two, grad_ffn_gain, grad_ffn_shift = layer_norm_backward(
        output_gradient, standardized_two, inverse_deviation_two, feedforward_norm_gain
    )
    grad_ffn_out = grad_sum_two.astype(jnp.bfloat16)
    grad_back_bias = jnp.sum(grad_ffn_out.astype(jnp.float32), 0)
    grad_back_mat = contract_rows(active_low, grad_ffn_out)
    grad_active = times_transposed(grad_ffn_out, back_mat)
    grad_inner = gelu_pullback(grad_active)[0].astype(jnp.bfloat16)
    grad_in_bias = jnp.sum(grad_inner.astype(jnp.float32), 0)
    grad_in_mat = contract_rows(normed_low, grad_inner)
    normalized_gradient = grad_sum_two + times_transposed(grad_inner, in_mat)
    grad_sum_one, grad_attn_gain, grad_attn_shift = layer_norm_backward(
        normalized_gradient, standardized_one, inverse_deviation_one, attention_norm_gain
    )
    grad_branch = grad_sum_one.astype(jnp.bfloat16)
    grad_out_bias = jnp.sum(grad_branch.astype(jnp.float32), 0)
    grad_out_mat = contract_rows(attended, grad_branch)
    grad_attended = times_transposed(grad_branch, out_mat).astype(jnp.bfloat16)
    grad_queries, row_delta, grad_keys_all, grad_values_all = attend_backward(
        query_rows, all_keys, all_values, grad_attended, log_total, same_doc
    )
    grad_keys, grad_values = (
        lax.psum_scatter(
            grad_keys_all.astype(jnp.bfloat16), "ctx", scatter_dimension=0, tiled=True
        ).astype(jnp.float32),
        lax.psum_scatter(
            grad_values_all.astype(jnp.bfloat16), "ctx", scatter_dimension=0, tiled=True
        ).astype(jnp.float32),
    )
    grad_query_low = grad_queries.astype(jnp.bfloat16)
    grad_key_low = grad_keys.astype(jnp.bfloat16)
    grad_value_low = grad_values.astype(jnp.bfloat16)
    grad_query_bias = jnp.sum(grad_query_low.astype(jnp.float32), 0)
    grad_value_bias = jnp.sum(grad_value_low.astype(jnp.float32), 0)
    grad_query_mat = contract_rows(inputs, grad_query_low)
    grad_key_mat = contract_rows(inputs, grad_key_low)
    grad_value_mat = contract_rows(inputs, grad_value_low)
    grad_inputs = (
        grad_sum_one
        + times_transposed(grad_query_low, query_mat)
        + times_transposed(grad_key_low, key_mat)
        + times_transposed(grad_value_low, value_mat)
    )
    local_grads = (
        grad_query_mat,
        grad_query_bias,
        grad_key_mat,
        grad_value_mat,
        grad_value_bias,
        grad_out_mat,
        grad_out_bias,
        grad_attn_gain,
        grad_attn_shift,
        grad_in_mat,
        grad_in_bias,
        grad_back_mat,
        grad_back_bias,
        grad_ffn_gain,
        grad_ffn_shift,
    )
    owned = (
        lax.psum_scatter(local_grads[0], ("ctx", "fsdp"), scatter_dimension=0, tiled=True),
        lax.psum_scatter(local_grads[1], ("ctx", "fsdp"), scatter_dimension=0, tiled=True),
        lax.psum_scatter(local_grads[2], ("ctx", "fsdp"), scatter_dimension=0, tiled=True),
        lax.psum_scatter(local_grads[3], ("ctx", "fsdp"), scatter_dimension=0, tiled=True),
        lax.psum_scatter(local_grads[4], ("ctx", "fsdp"), scatter_dimension=0, tiled=True),
        lax.psum_scatter(local_grads[5], ("ctx", "fsdp"), scatter_dimension=0, tiled=True),
        lax.psum_scatter(local_grads[6], ("ctx", "fsdp"), scatter_dimension=0, tiled=True),
        lax.psum_scatter(local_grads[7], ("ctx", "fsdp"), scatter_dimension=0, tiled=True),
        lax.psum_scatter(local_grads[8], ("ctx", "fsdp"), scatter_dimension=0, tiled=True),
        lax.psum_scatter(local_grads[9], ("ctx", "fsdp"), scatter_dimension=0, tiled=True),
        lax.psum_scatter(local_grads[10], ("ctx", "fsdp"), scatter_dimension=0, tiled=True),
        lax.psum_scatter(local_grads[11], ("ctx", "fsdp"), scatter_dimension=0, tiled=True),
        lax.psum_scatter(local_grads[12], ("ctx", "fsdp"), scatter_dimension=0, tiled=True),
        lax.psum_scatter(local_grads[13], ("ctx", "fsdp"), scatter_dimension=0, tiled=True),
        lax.psum_scatter(local_grads[14], ("ctx", "fsdp"), scatter_dimension=0, tiled=True),
    )
    summed = (
        lax.psum(owned[0].astype(jnp.bfloat16), "dp").astype(jnp.float32),
        lax.psum(owned[1].astype(jnp.bfloat16), "dp").astype(jnp.float32),
        lax.psum(owned[2].astype(jnp.bfloat16), "dp").astype(jnp.float32),
        lax.psum(owned[3].astype(jnp.bfloat16), "dp").astype(jnp.float32),
        lax.psum(owned[4].astype(jnp.bfloat16), "dp").astype(jnp.float32),
        lax.psum(owned[5].astype(jnp.bfloat16), "dp").astype(jnp.float32),
        lax.psum(owned[6].astype(jnp.bfloat16), "dp").astype(jnp.float32),
        lax.psum(owned[7].astype(jnp.bfloat16), "dp").astype(jnp.float32),
        lax.psum(owned[8].astype(jnp.bfloat16), "dp").astype(jnp.float32),
        lax.psum(owned[9].astype(jnp.bfloat16), "dp").astype(jnp.float32),
        lax.psum(owned[10].astype(jnp.bfloat16), "dp").astype(jnp.float32),
        lax.psum(owned[11].astype(jnp.bfloat16), "dp").astype(jnp.float32),
        lax.psum(owned[12].astype(jnp.bfloat16), "dp").astype(jnp.float32),
        lax.psum(owned[13].astype(jnp.bfloat16), "dp").astype(jnp.float32),
        lax.psum(owned[14].astype(jnp.bfloat16), "dp").astype(jnp.float32),
    )
    return (
        norm_result.astype(jnp.bfloat16)[None],
        grad_inputs[None],
        summed[0],
        summed[1],
        summed[2],
        summed[3],
        summed[4],
        summed[5],
        summed[6],
        summed[7],
        summed[8],
        summed[9],
        summed[10],
        summed[11],
        summed[12],
        summed[13],
        summed[14],
    )


def solution(mesh):
    placed = (
        P(("dp", "fsdp"), "ctx", None),
        P(("dp", "fsdp"), "ctx"),
        P(("ctx", "fsdp"), None),
        P(("ctx", "fsdp")),
        P(("ctx", "fsdp"), None),
        P(("ctx", "fsdp"), None),
        P(("ctx", "fsdp")),
        P(("ctx", "fsdp"), None),
        P(("ctx", "fsdp")),
        P(("ctx", "fsdp")),
        P(("ctx", "fsdp")),
        P(("ctx", "fsdp"), None),
        P(("ctx", "fsdp")),
        P(("ctx", "fsdp"), None),
        P(("ctx", "fsdp")),
        P(("ctx", "fsdp")),
        P(("ctx", "fsdp")),
        P(("dp", "fsdp"), "ctx", None),
    )
    return jax.shard_map(
        body,
        mesh=mesh,
        in_specs=placed,
        out_specs=(
            P(("dp", "fsdp"), "ctx", None),
            P(("dp", "fsdp"), "ctx", None),
            P(("ctx", "fsdp"), None),
            P(("ctx", "fsdp")),
            P(("ctx", "fsdp"), None),
            P(("ctx", "fsdp"), None),
            P(("ctx", "fsdp")),
            P(("ctx", "fsdp"), None),
            P(("ctx", "fsdp")),
            P(("ctx", "fsdp")),
            P(("ctx", "fsdp")),
            P(("ctx", "fsdp"), None),
            P(("ctx", "fsdp")),
            P(("ctx", "fsdp"), None),
            P(("ctx", "fsdp")),
            P(("ctx", "fsdp")),
            P(("ctx", "fsdp")),
        ),
        check_vma=False,
    )
```

profile of v0, /device:TPU:0, one launch (start us, length us, event | category | flops | bytes accessed | tf_op | source)
XLA Modules:
  0.0 2166.8 jit_solution(9182918693039032137)
XLA Ops:
  18.2 79.0 %all-reduce.18 = (bf16[1024]{0:T(1024)(128)(2,1)S(1)}, bf16[1024]{0:T(1024)(128)(2,1)S(1)}, bf16[1024]{0:T(1024)(128)(2,1)S(1)}, bf16[1024]{0:T(1024)(128)(2,1)S...) all-reduce(bf16[1024]{0:T(1024)(128)(2,1)S(1)} %dynamic-update-slic, ...), channel_id=1, replica_groups=mesh['dp'=2,'ctx'=8,'fsdp'=2] {'ctx','fsdp'}, use_global_device_ids=true, to_apply=%add.1 | all-reduce | flops 8192 | bytes 32768
  97.2 3.3 fusion.25
  100.6 36.2 %all-gather.17.cloned.1.call-done = bf16[1024,1024]{1,0:T(8,128)(2,1)} async-done(((bf16[64,1024]{1,0:T(8,128)(2,1)}), bf16[1024,1024]{1,0:T(8,128)(2,1)}) %all-gather.17.cloned.1.call-update) | async-done | bytes 2097168 | tf_op jit(solution)/shard_map/all_gather | solution.py:211
  136.8 3.1 convolution_convert_fusion.1
  142.1 38.4 %all-gather.1 = bf16[16,1,256]{2,1,0:T(2,128)(2,1)S(1)} all-gather(bf16[1,1,256]{2,1,0:T(2,128)(2,1)S(1)} %reshape.206), channel_id=1, replica_groups=mesh['dp'=2,'ctx'=8,'fsdp'=2] {'ctx','fsdp'}, dimensions={0}, use_global_device_ids=true | all-gather | bytes 8704 | tf_op jit(solution)/shard_map/all_gather | solution.py:219
  180.5 16.7 all-gather
  199.1 2.3 fusion.26
  201.6 72.1 %all-gather.13.cloned.1.call-done = bf16[2048,1024]{1,0:T(8,128)(2,1)} async-done(((bf16[256,1024]{1,0:T(8,128)(2,1)}), bf16[2048,1024]{1,0:T(8,128)(2,1)}) %all-gather.13.cloned.1.call-update) | async-done | bytes 4194320 | tf_op jit(solution)/shard_map/all_gather | solution.py:253
  273.7 6.5 copy.45
  280.2 67.8 %all-gather.19.cloned.1.call-done = bf16[2048,1024]{1,0:T(8,128)(2,1)} async-done(((bf16[256,1024]{1,0:T(8,128)(2,1)}), bf16[2048,1024]{1,0:T(8,128)(2,1)}) %all-gather.19.cloned.1.call-update) | async-done | bytes 4194320 | tf_op jit(solution)/shard_map/all_gather | solution.py:252
  347.9 6.5 copy.47
  354.5 42.6 %while.34 = (s32[]{:T(128)}, bf16[256,1024]{0,1:T(8,128)(2,1)S(1)}, f32[16,256]{1,0:T(8,128)S(1)}, bf16[2048,1024]{0,1:T(8,128)(2,1)}, bf16[256,1024]{0,1:T(8,12...) while((s32[]{:T(128)}, bf16[256,1024]{0,1:T(8,128)(2,1)S(1)}, ...), condition=%wide.region_3.4_spmd.clone, body=%wide.region_0.3_spmd.clone.sunk | while | flops 281542144 | bytes 18240248 | solution.py:99
  397.2 12.4 all-gather.21.cloned.1.call-done
  409.6 2.4 fusion.58
  412.3 111.6 %all-gather.23.cloned.1.call-done = bf16[1024,4096]{1,0:T(8,128)(2,1)} async-done(((bf16[64,4096]{1,0:T(8,128)(2,1)}), bf16[1024,4096]{1,0:T(8,128)(2,1)}) %all-gather.23.cloned.1.call-update) | async-done | bytes 8388624 | tf_op jit(solution)/shard_map/all_gather | solution.py:218
  523.8 16.2 multiply_convert_fusion.1
  540.0 97.6 %all-gather.25.cloned.1.call-done = bf16[4096,1024]{1,0:T(8,128)(2,1)} async-done(((bf16[256,1024]{1,0:T(8,128)(2,1)}), bf16[4096,1024]{1,0:T(8,128)(2,1)}) %all-gather.25.cloned.1.call-update) | async-done | bytes 8388624 | tf_op jit(solution)/shard_map/all_gather | solution.py:220
  637.7 6.6 fusion.59
  646.4 6.5 convert_reduce_fusion
  653.0 6.9 multiply_reduce_fusion.1
  661.8 2.5 broadcast.133
  664.3 2.5 broadcast.133.clone
  666.8 114.8 %while.35 = (s32[]{:T(128)}, bf16[256,1024]{0,1:T(8,128)(2,1)S(1)}, bf16[2048,1024]{0,1:T(8,128)(2,1)}, bf16[2048,1024]{0,1:T(8,128)(2,1)}, bf16[2048,1024]{0,1:...) while((s32[]{:T(128)}, bf16[256,1024]{0,1:T(8,128)(2,1)S(1)}, ...), condition=%wide.region_14.15_spmd.clone, body=%wide.region_12.0_spmd.clone.sunk | while | flops 681639424 | bytes 56965944 | solution.py:168
  670.3 2.7 fusion.131
  674.2 4.0 multiply_reduce_fusion.7
  684.7 2.7 fusion.131
  688.6 4.0 multiply_reduce_fusion.7
  699.0 2.7 fusion.131
  702.9 4.0 multiply_reduce_fusion.7
  713.3 2.7 fusion.131
  717.2 4.0 multiply_reduce_fusion.7
  727.6 2.7 fusion.131
  731.5 4.0 multiply_reduce_fusion.7
  741.9 2.7 fusion.131
  745.8 4.0 multiply_reduce_fusion.7
  756.2 2.7 fusion.131
  760.1 4.0 multiply_reduce_fusion.7
  770.4 2.7 fusion.131
  774.3 4.0 multiply_reduce_fusion.7
  782.6 2.6 convolution_bitcast_fusion.2
  785.3 5.4 copy.55
  790.8 3.7 fusion.39
  794.6 73.9 %reduce-scatter.15.cloned.1.call-done = bf16[256,1024]{0,1:T(8,128)(2,1)} async-done(((bf16[2048,1024]{0,1:T(8,128)(2,1)}), bf16[256,1024]{0,1:T(8,128)(2,1)}) %reduce-scatter.15.cloned.1.call-update) | async-done | bytes 524304 | tf_op jit(solution)/shard_map/reduce_scatter | solution.py:296
  868.4 3.7 convolution_bitcast_fusion.1
  872.1 5.3 copy.57
  877.5 83.1 %reduce-scatter.17.cloned.1.call-done = bf16[256,1024]{0,1:T(8,128)(2,1)} async-done(((bf16[2048,1024]{0,1:T(8,128)(2,1)}), bf16[256,1024]{0,1:T(8,128)(2,1)}) %reduce-scatter.17.cloned.1.call-update) | async-done | bytes 524304 | tf_op jit(solution)/shard_map/reduce_scatter | solution.py:299
  960.6 3.7 convolution_bitcast_fusion
  964.3 5.3 copy.59
  969.7 9.8 fusion.52
  980.7 9.7 fusion.46
  990.5 67.3 %reduce-scatter.25.cloned.1.call-done = f32[64,1024]{1,0:T(8,128)} async-done(((f32[1024,1024]{1,0:T(8,128)}), f32[64,1024]{1,0:T(8,128)}) %reduce-scatter.25.cloned.1.call-update) | async-done | bytes 262160
  1059.6 95.1 %reduce-scatter.19.cloned.1.call-done = f32[64,1024]{1,0:T(8,128)} async-done(((f32[1024,1024]{1,0:T(8,128)}), f32[64,1024]{1,0:T(8,128)}) %reduce-scatter.19.cloned.1.call-update) | async-done | bytes 262160 | tf_op jit(solution)/shard_map/reduce_scatter | solution.py:340
  1156.3 95.4 %reduce-scatter.27.cloned.1.call-done = f32[64,1024]{1,0:T(8,128)} async-done(((f32[1024,1024]{1,0:T(8,128)}), f32[64,1024]{1,0:T(8,128)}) %reduce-scatter.27.cloned.1.call-update) | async-done | bytes 262160
  1253.6 95.1 %reduce-scatter.29.cloned.1.call-done = f32[64,1024]{1,0:T(8,128)} async-done(((f32[1024,1024]{1,0:T(8,128)}), f32[64,1024]{1,0:T(8,128)}) %reduce-scatter.29.cloned.1.call-update) | async-done | bytes 262160
  1350.5 346.4 %reduce-scatter.21.cloned.1.call-done = f32[64,4096]{1,0:T(8,128)} async-done(((f32[1024,4096]{1,0:T(8,128)}), f32[64,4096]{1,0:T(8,128)}) %reduce-scatter.21.cloned.1.call-update) | async-done | bytes 1048592 | tf_op jit(solution)/shard_map/reduce_scatter | solution.py:344
  1696.8 2.1 convert_element_type.269
  1698.9 352.1 %reduce-scatter.23.cloned.1.call-done = f32[256,1024]{1,0:T(8,128)} async-done(((f32[4096,1024]{1,0:T(8,128)}), f32[256,1024]{1,0:T(8,128)}) %reduce-scatter.23.cloned.1.call-update) | async-done | bytes 1048592 | tf_op jit(solution)/shard_map/reduce_scatter | solution.py:346
  2051.0 2.1 convert_element_type.274
  2054.8 2.3 convolution_add_fusion.3
  2057.4 79.4 %all-reduce.17 = (bf16[1024]{0:T(1024)(128)(2,1)S(1)}, bf16[1024]{0:T(1024)(128)(2,1)S(1)}, bf16[1024]{0:T(1024)(128)(2,1)S(1)}, bf16[1024]{0:T(1024)(128)(2,1)S...) all-reduce(f32[1024]{0:T(1024)S(1)} %convert_reduce_fusion.5, ...), channel_id=6, replica_groups=mesh['dp'=2,'ctx'=8,'fsdp'=2] {'ctx','fsdp'}, use_global_device_ids=true, to_apply=%region_20.0.clone | all-reduce | flops 12288 | bytes 73728
  2137.5 2.5 all-reduce.19
  2144.6 2.5 convolution_add_fusion.2
  2155.8 2.1 convert_element_type.270
  2157.9 2.1 convert_element_type.275
  (331 shorter events, 145.2 us)
Async XLA Ops:
  7.2 129.6 %copy-start.1 = (bf16[1,256,1024]{2,1,0:T(8,128)(2,1)S(1)}, bf16[1,256,1024]{2,1,0:T(8,128)(2,1)}, u32[]{:S(2)}) copy-start(bf16[1,256,1024]{2,1,0:T(8,128)(2,1)} %param.22) | copy-start | bytes 1572868
  7.2 90.0 %all-gather.11.cloned.1.call-start = ((), (), s32[]{:S(2)}) async-start(), calls=%async_computation.8 | async-start | bytes 2228224 | tf_op jit(solution)/shard_map/all_gather | solution.py:212
  7.9 128.9 %all-gather.17.cloned.1.call-start = ((), (), s32[]{:S(2)}) async-start(), calls=%async_computation.11 | async-start | bytes 2228224 | tf_op jit(solution)/shard_map/all_gather | solution.py:211
  8.7 190.4 %all-gather.15.cloned.1.call-start = ((), (), s32[]{:S(2)}) async-start(), calls=%async_computation.10 | async-start | bytes 2228224 | tf_op jit(solution)/shard_map/all_gather | solution.py:209
  9.4 264.3 %all-gather.13.cloned.1.call-start = ((), (), s32[]{:S(2)}) async-start(), calls=%async_computation.9 | async-start | bytes 4718592 | tf_op jit(solution)/shard_map/all_gather | solution.py:253
  97.2 44.9 %copy-start.13 = (s32[1,256]{1,0:T(1,128)S(1)}, s32[1,256]{1,0:T(1,128)}, u32[]{:S(2)}) copy-start(s32[1,256]{1,0:T(1,128)} %param.23) | copy-start | bytes 3076
  97.2 44.9 %copy-start.14 = (bf16[256]{0:T(256)(128)(2,1)S(1)}, bf16[256]{0:T(256)(128)(2,1)}, u32[]{:S(2)}) copy-start(bf16[256]{0:T(256)(128)(2,1)} %param.34) | copy-start | bytes 1540
  100.5 247.4 %all-gather.19.cloned.1.call-start = ((), (), s32[]{:S(2)}) async-start(), calls=%async_computation.12 | async-start | bytes 4718592 | tf_op jit(solution)/shard_map/all_gather | solution.py:252
  139.9 269.6 %all-gather.21.cloned.1.call-start = ((), (), s32[]{:S(2)}) async-start(), calls=%async_computation.13 | async-start | bytes 2228224 | tf_op jit(solution)/shard_map/all_gather | solution.py:214
  140.5 383.3 %all-gather.23.cloned.1.call-start = ((), (), s32[]{:S(2)}) async-start(), calls=%async_computation.14 | async-start | bytes 8912896 | tf_op jit(solution)/shard_map/all_gather | solution.py:218
  141.2 496.4 %all-gather.25.cloned.1.call-start = ((), (), s32[]{:S(2)}) async-start(), calls=%async_computation.15 | async-start | bytes 8912896 | tf_op jit(solution)/shard_map/all_gather | solution.py:220
  142.0 726.4 %reduce-scatter.15.cloned.1.call-start = ((), (), s32[]{:S(2)}) async-start(), calls=%async_computation.16 | async-start | bytes 4718592 | tf_op jit(solution)/shard_map/reduce_scatter | solution.py:296
  397.1 12.4 copy-start.10
  397.1 142.9 %copy-start.7 = (bf16[256,1024]{0,1:T(8,128)(2,1)}, bf16[256,1024]{0,1:T(8,128)(2,1)S(1)}, u32[]{:S(2)}) copy-start(bf16[256,1024]{0,1:T(8,128)(2,1)S(1)} %get-tuple-element.313) | copy-start | bytes 1572868
  637.7 8.7 slice-start
  637.7 6.9 copy-start.5
  637.7 8.7 slice-start.1
  646.4 6.6 copy-start.8
  652.9 6.9 copy-start.12
  653.0 7.3 copy-start.3
  674.2 4.0 copy-start
  688.5 4.0 copy-start
  702.9 4.0 copy-start
  717.2 4.0 copy-start
  731.4 4.0 copy-start
  745.8 4.0 copy-start
  760.0 4.0 copy-start
  774.3 4.0 copy-start
  781.6 1.0 copy-start.2
  781.6 179.0 %reduce-scatter.17.cloned.1.call-start = ((), (), s32[]{:S(2)}) async-start(), calls=%async_computation.17 | async-start | bytes 4718592 | tf_op jit(solution)/shard_map/reduce_scatter | solution.py:299
  782.2 275.6 %reduce-scatter.25.cloned.1.call-start = ((), (), s32[]{:S(2)}) async-start(), calls=%async_computation.21 | async-start | bytes 4456448
  790.7 364.0 %reduce-scatter.19.cloned.1.call-start = ((), (), s32[]{:S(2)}) async-start(), calls=%async_computation.18 | async-start | bytes 4456448 | tf_op jit(solution)/shard_map/reduce_scatter | solution.py:340
  794.5 457.3 %reduce-scatter.27.cloned.1.call-start = ((), (), s32[]{:S(2)}) async-start(), calls=%async_computation.22 | async-start | bytes 4456448
  877.5 471.2 %reduce-scatter.29.cloned.1.call-start = ((), (), s32[]{:S(2)}) async-start(), calls=%async_computation.23 | async-start | bytes 4456448
  969.6 727.2 %reduce-scatter.21.cloned.1.call-start = ((), (), s32[]{:S(2)}) async-start(), calls=%async_computation.19 | async-start | bytes 17825792 | tf_op jit(solution)/shard_map/reduce_scatter | solution.py:344
  979.5 1.2 copy-start.9
  979.5 1071.5 %reduce-scatter.23.cloned.1.call-start = ((), (), s32[]{:S(2)}) async-start(), calls=%async_computation.20 | async-start | bytes 17825792 | tf_op jit(solution)/shard_map/reduce_scatter | solution.py:346
  990.5 1064.0 %copy-start.6 = (bf16[1,256,1024]{2,1,0:T(8,128)(2,1)S(1)}, bf16[1,256,1024]{2,1,0:T(8,128)(2,1)}, u32[]{:S(2)}) copy-start(bf16[1,256,1024]{2,1,0:T(8,128)(2,1)} %param.39) | copy-start | bytes 1572868
  990.5 1158.4 %all-reduce.23.cloned.1.call-start = ((), (), s32[]{:S(2)}) async-start(), calls=%async_computation.24 | async-start | bytes 3932160 | tf_op jit(solution)/shard_map/psum | solution.py:352
  2053.1 4.1 copy-start.4
  2139.9 7.2 copy-start.11
Sparse Core Ops, SparseCore 0:
  10.8 64.1 all-gather.10
  77.8 58.9 all-gather.16
  139.6 59.4 all-gather.14
  201.6 72.0 all-gather.12
  276.2 71.6 all-gather.18
  350.6 58.9 all-gather.20
  412.3 111.4 all-gather.22
  526.6 111.0 all-gather.24
  781.7 86.6 reduce-scatter.14
  872.3 88.2 reduce-scatter.16
  962.9 94.8 reduce-scatter.24
  1059.9 94.7 reduce-scatter.18
  1157.0 94.7 reduce-scatter.26
  1253.9 94.7 reduce-scatter.28
  1350.8 345.9 reduce-scatter.20
  1699.0 351.9 reduce-scatter.22
  2054.8 26.9 all-reduce.22
where the time goes:
time: 2170 us
  waiting for transfers between devices  1610 us (74%)
  blocking collectives  216 us (10%)
  matrix products  175 us (8%)
  local copies, waits for them, and re-layouts  106 us (5%)
  other arithmetic  38.4 us (2%)
    reduce_scatter x1, waiting for transfers between devices, body(): lax.psum_scatter(local_grads[11], ('ctx', 'fsdp'), scatter_dimension=0, t...  352 us
    reduce_scatter x1, waiting for transfers between devices, body(): lax.psum_scatter(local_grads[9], ('ctx', 'fsdp'), scatter_dimension=0, ti...  346 us
    unnamed x20, waiting for transfers between devices  262 us
    unnamed x2, blocking collectives  158 us
    all_gather x1, waiting for transfers between devices, body(): lax.all_gather(shards[9], ('ctx', 'fsdp'), axis=0, tiled=True)  112 us
    all_gather x1, waiting for transfers between devices, body(): lax.all_gather(shards[11], ('ctx', 'fsdp'), axis=0, tiled=True)  97.6 us
    reduce_scatter x1, waiting for transfers between devices, body(): lax.psum_scatter(local_grads[5], ('ctx', 'fsdp'), scatter_dimension=0, ti...  95.1 us
    reduce_scatter x1, waiting for transfers between devices, body(): lax.psum_scatter(grad_values_all.astype(jnp.bfloat16), 'ctx', scatter_dim...  83.1 us
  transfers between devices with their start and end apart: 17, of which 15 were waited for; matrix products, arithmetic and copies ran while one was open for 7% of the time, Pallas kernels for 0%

commit v1 on v0

v1 whole, which is shorter than its diff:
```python
from functools import partial

import jax
import jax.numpy as jnp
import numpy as np
from jax import lax
from jax.experimental import pallas as pl
from jax.experimental.pallas import tpu as pltpu
from jax.sharding import PartitionSpec as P

D = 1024
H = 16
HD = 64
FF = 4096
NORM_EPS = 1e-05
NEG_FILL = -1e30
AXES = ("dp", "ctx", "fsdp")
BF = jnp.bfloat16
F32 = jnp.float32
VMEM_LIMIT = 48 * 1024 * 1024


def subset_masks(order):
    table = [0]
    for mask in order:
        table = table + [mask ^ entry for entry in table]
    return table


def bits_of(count):
    return [1 << t for t in range(count.bit_length() - 1)]


class Plan:
    def __init__(self, mesh):
        self.ctx = mesh.shape["ctx"]
        self.fsdp = mesh.shape["fsdp"]
        self.chips = self.ctx * self.fsdp
        self.groups = self.ctx // 2
        self.heads = H // self.ctx
        self.devices = [
            (c, j, f) for c in range(2) for j in range(self.ctx) for f in range(self.fsdp)
        ]
        bits = bits_of(self.chips)
        self.chip_orders = [bits[2:] + [1, 2], bits[2:] + [2, 1]]
        self.chip_masks = [subset_masks(order) for order in self.chip_orders]
        group_bits = bits_of(self.groups)
        self.group_orders = [group_bits[::-1], group_bits]
        self.group_masks = [subset_masks(order) for order in self.group_orders]
        top = self.groups * self.fsdp
        self.side_orders = [bits_of(self.fsdp) + [top], [top] + bits_of(self.fsdp)]
        self.side_masks = [subset_masks(order) for order in self.side_orders]

    def flat(self, c, j, f):
        return (c * self.ctx + j) * self.fsdp + f

    def perm(self, move):
        return [(self.flat(*dev), self.flat(*move(*dev))) for dev in self.devices]

    def chip_xor(self, masks):
        def move(c, j, f):
            i = (j * self.fsdp + f) ^ masks[c]
            return (c, i // self.fsdp, i % self.fsdp)

        return self.perm(move)

    def chip_perms(self):
        return [self.chip_xor(pair) for pair in zip(*self.chip_orders)]

    def side_perms(self):
        return [self.chip_xor(pair) for pair in zip(*self.side_orders)]

    def group_perms(self):
        return [
            self.perm(lambda c, j, f, pair=pair: (c, j ^ pair[c], f))
            for pair in zip(*self.group_orders)
        ]

    def group_direct(self, d):
        return self.perm(lambda c, j, f: (c, j ^ d, f))

    def core_swap(self):
        return self.perm(lambda c, j, f: (1 - c, j, f))

    def turn(self):
        def move(c, j, f):
            return (j // self.groups, c * self.groups + j % self.groups, f)

        return self.perm(move)

    def chunk_of(self, c, j, p):
        e, k = divmod(p, self.groups)
        return (c ^ e) * self.groups + ((j % self.groups) ^ self.group_masks[c ^ e][k])

    def outward(self, p):
        def move(c, j, f):
            return (j // self.groups, self.chunk_of(c, j, p), f)

        return self.perm(move)

    def inward(self, p):
        return [(b, a) for a, b in self.outward(p)]

    def head_block(self, c, j, p):
        e, k = divmod(p, self.groups)
        s, g = divmod(j, self.groups)
        return (s ^ e) * self.groups + (g ^ self.group_masks[s][k])

    def table(self, entries):
        return np.array([entries(*dev) for dev in self.devices], np.int32)

    def chip_gather(self):
        def entries(c, j, f):
            inverse = np.argsort(self.chip_masks[c])
            return [inverse[(j * self.fsdp + f) ^ i] for i in range(self.chips)]

        return self.table(entries)

    def chip_spread(self):
        return self.table(
            lambda c, j, f: [(j * self.fsdp + f) ^ mask for mask in self.chip_masks[c]]
        )

    def out_rows(self, rows):
        per = self.heads * HD // rows

        def entries(c, j, f):
            return [
                self.head_block(c, j, p) * per + t for p in range(self.ctx) for t in range(per)
            ]

        return self.table(entries)

    def side_pieces(self):
        def entries(c, j, f):
            return [
                (j * self.fsdp + f) ^ mask ^ (d * self.fsdp)
                for mask in self.side_masks[c]
                for d in range(self.groups)
            ]

        return self.table(entries)


def invert(table):
    return np.argsort(table, axis=1).astype(np.int32)


def route(sources, table, outs, moves):
    def kernel(table_ref, *refs):
        ins, results, sems = refs[: len(sources)], refs[len(sources) : -1], refs[-1]

        def copy(m, source, piece):
            _, _, row, rows, out, out_piece, out_row = moves[m]
            return pltpu.make_async_copy(
                source.at[piece, pl.ds(row, rows)],
                results[out].at[out_piece, pl.ds(out_row, rows)],
                sems.at[m],
            )

        for m, (group, slot, *_) in enumerate(moves):
            index = table_ref[slot]
            start = 0
            for which in group:
                count = sources[which].shape[0]

                @pl.when((index >= start) & (index < start + count))
                def _():
                    copy(m, ins[which], index - start).start()

                start += count
        for m, (group, *_) in enumerate(moves):
            copy(m, ins[group[0]], 0).wait()

    total = sum(
        moves[m][3] * outs[moves[m][4]].shape[2] * outs[moves[m][4]].dtype.itemsize
        for m in range(len(moves))
    )
    return pl.pallas_call(
        kernel,
        out_shape=outs,
        in_specs=[pl.BlockSpec(memory_space=pltpu.SMEM)]
        + [pl.BlockSpec(memory_space=pl.ANY)] * len(sources),
        out_specs=[pl.BlockSpec(memory_space=pltpu.VMEM)] * len(outs),
        scratch_shapes=[pltpu.SemaphoreType.DMA((len(moves),))],
        compiler_params=pltpu.CompilerParams(vmem_limit_bytes=VMEM_LIMIT),
        cost_estimate=pl.CostEstimate(flops=0, bytes_accessed=2 * total, transcendentals=0),
    )(table, *sources)


def nt(left, right):
    return lax.dot_general(left, right, (((1,), (1,)), ((), ())), preferred_element_type=F32)


def nn(left, right):
    return lax.dot_general(left, right, (((1,), (0,)), ((), ())), preferred_element_type=F32)


def tn(left, right):
    return lax.dot_general(left, right, (((0,), (0,)), ((), ())), preferred_element_type=F32)


def column_ids(row):
    return jnp.transpose(jnp.broadcast_to(row, (128, row.shape[1])))


def attend_forward(qkv_own, qkv_other, ids, overlap, heads):
    half, rows, width = qkv_own.shape
    chunks = 2 * half
    lanes = heads * HD

    def kernel(overlap_ref, own_ref, other_ref, ids_ref, *refs):
        outs = refs[:chunks]
        flat_ref, total_ref, keys, values, queries, cols, high, low, acc = refs[chunks:]
        step = pl.program_id(0)

        @pl.when(step == 0)
        def _():
            for p in range(chunks):
                block = (own_ref if p < half else other_ref)[p % half]
                queries[p] = block[:, :lanes] * BF(HD**-0.5)
                keys[p] = block[:, lanes : 2 * lanes]
                values[p] = jnp.transpose(block[:, 2 * lanes :])
                cols[p] = column_ids(ids_ref[p])

        high[...] = jnp.full_like(high, NEG_FILL)
        low[...] = jnp.zeros_like(low)
        acc[...] = jnp.zeros_like(acc)
        query = queries[step]
        row_ids = ids_ref[step]

        def one(p, carry):
            @pl.when(overlap_ref[step, p] > 0)
            def _():
                same = (
                    jnp.concatenate([cols[p]] * (-(-rows // 128)), axis=1)[:, :rows] == row_ids
                )
                key = keys[p]
                for h in range(heads):
                    at = slice(h * HD, (h + 1) * HD)
                    logits = jnp.where(same, nt(key[:, at], query[:, at]), NEG_FILL)
                    before = high[h : h + 1]
                    now = jnp.maximum(before, jnp.max(logits, 0, keepdims=True))
                    weights = jnp.exp(logits - now)
                    fade = jnp.exp(before - now)
                    high[h : h + 1] = now
                    low[h : h + 1] = low[h : h + 1] * fade + jnp.sum(weights, 0, keepdims=True)
                    acc[at] = acc[at] * fade + nn(values[p, at], weights.astype(BF))

            return carry

        lax.fori_loop(0, chunks, one, 0)
        flat = jnp.concatenate(
            [acc[h * HD : (h + 1) * HD] / low[h : h + 1] for h in range(heads)], axis=0
        )
        flat_ref[0] = flat
        total_ref[0] = high[...] + jnp.log(jnp.maximum(low[...], 1e-30))
        turned = jnp.transpose(flat).astype(BF)
        for p in range(chunks):

            @pl.when(step == p)
            def _():
                outs[p][...] = turned

    whole = lambda *shape: pl.BlockSpec(shape, lambda i, o: (0,) * len(shape))
    pairs = chunks * chunks * heads
    return pl.pallas_call(
        kernel,
        out_shape=[jax.ShapeDtypeStruct((rows, lanes), BF)] * chunks
        + [
            jax.ShapeDtypeStruct((chunks, lanes, rows), F32),
            jax.ShapeDtypeStruct((chunks, 8, rows), F32),
        ],
        grid_spec=pltpu.PrefetchScalarGridSpec(
            num_scalar_prefetch=1,
            grid=(chunks,),
            in_specs=[
                whole(half, rows, width),
                whole(half, rows, width),
                whole(chunks, 1, rows),
            ],
            out_specs=[whole(rows, lanes)] * chunks
            + [
                pl.BlockSpec((1, lanes, rows), lambda i, o: (i, 0, 0)),
                pl.BlockSpec((1, 8, rows), lambda i, o: (i, 0, 0)),
            ],
            scratch_shapes=[
                pltpu.VMEM((chunks, rows, lanes), BF),
                pltpu.VMEM((chunks, lanes, rows), BF),
                pltpu.VMEM((chunks, rows, lanes), BF),
                pltpu.VMEM((chunks, rows, 128), F32),
                pltpu.VMEM((8, rows), F32),
                pltpu.VMEM((8, rows), F32),
                pltpu.VMEM((lanes, rows), F32),
            ],
        ),
        compiler_params=pltpu.CompilerParams(vmem_limit_bytes=VMEM_LIMIT),
        cost_estimate=pl.CostEstimate(
            flops=pairs * rows * rows * 256,
            bytes_accessed=chunks * rows * width * 4,
            transcendentals=pairs * rows * rows,
        ),
    )(overlap, qkv_own, qkv_other, ids)


def attend_backward(qkv_own, qkv_other, ids, overlap, grads, flat, totals, heads):
    half, rows, width = qkv_own.shape
    chunks = 2 * half
    lanes = heads * HD

    def kernel(overlap_ref, own_ref, other_ref, ids_ref, flat_ref, total_ref, *refs):
        grad_refs = refs[:chunks]
        down_own, down_other = refs[chunks : chunks + 2]
        keys, turned, values, queries, ups, cols, grad_key, grad_value, acc = refs[chunks + 2 :]
        step = pl.program_id(0)

        @pl.when(step == 0)
        def _():
            for p in range(chunks):
                block = (own_ref if p < half else other_ref)[p % half]
                queries[p] = block[:, :lanes] * BF(HD**-0.5)
                keys[p] = block[:, lanes : 2 * lanes]
                turned[p] = jnp.transpose(block[:, lanes : 2 * lanes])
                values[p] = block[:, 2 * lanes :]
                ups[p] = grad_refs[p][...]
                cols[p] = column_ids(ids_ref[p])
            grad_key[...] = jnp.zeros_like(grad_key)
            grad_value[...] = jnp.zeros_like(grad_value)

        query = queries[step]
        row_ids = ids_ref[step]
        up = ups[step]
        product = jnp.transpose(up.astype(F32)) * flat_ref[0]
        deltas = [
            jnp.sum(product[h * HD : (h + 1) * HD], 0, keepdims=True) for h in range(heads)
        ]
        total = total_ref[0]
        acc[...] = jnp.zeros_like(acc)

        def one(p, carry):
            @pl.when(overlap_ref[step, p] > 0)
            def _():
                same = (
                    jnp.concatenate([cols[p]] * (-(-rows // 128)), axis=1)[:, :rows] == row_ids
                )
                key, value = keys[p], values[p]
                key_parts, value_parts = [], []
                for h in range(heads):
                    at = slice(h * HD, (h + 1) * HD)
                    logits = jnp.where(same, nt(key[:, at], query[:, at]), NEG_FILL)
                    weights = jnp.exp(logits - total[h : h + 1])
                    grad_prob = nt(value[:, at], up[:, at])
                    grad_score = (weights * (grad_prob - deltas[h])).astype(BF)
                    value_parts.append(nn(weights.astype(BF), up[:, at]))
                    key_parts.append(nn(grad_score, query[:, at]))
                    acc[at] = acc[at] + nn(turned[p, at], grad_score)
                grad_value[p] = grad_value[p] + jnp.concatenate(value_parts, axis=1)
                grad_key[p] = grad_key[p] + jnp.concatenate(key_parts, axis=1)

            return carry

        lax.fori_loop(0, chunks, one, 0)
        grad_query = (jnp.transpose(acc[...]) * HD**-0.5).astype(BF)
        for p in range(chunks):
            out = down_own if p < half else down_other

            @pl.when(step == p)
            def _():
                out[p % half, :, :lanes] = grad_query

            @pl.when(step == chunks - 1)
            def _():
                out[p % half, :, lanes : 2 * lanes] = grad_key[p].astype(BF)
                out[p % half, :, 2 * lanes :] = grad_value[p].astype(BF)

    whole = lambda *shape: pl.BlockSpec(shape, lambda i, o: (0,) * len(shape))
    pairs = chunks * chunks * heads
    return pl.pallas_call(
        kernel,
        out_shape=[jax.ShapeDtypeStruct((half, rows, width), BF)] * 2,
        grid_spec=pltpu.PrefetchScalarGridSpec(
            num_scalar_prefetch=1,
            grid=(chunks,),
            in_specs=[
                whole(half, rows, width),
                whole(half, rows, width),
                whole(chunks, 1, rows),
                pl.BlockSpec((1, lanes, rows), lambda i, o: (i, 0, 0)),
                pl.BlockSpec((1, 8, rows), lambda i, o: (i, 0, 0)),
            ]
            + [whole(rows, lanes)] * chunks,
            out_specs=[whole(half, rows, width)] * 2,
            scratch_shapes=[
                pltpu.VMEM((chunks, rows, lanes), BF),
                pltpu.VMEM((chunks, lanes, rows), BF),
                pltpu.VMEM((chunks, rows, lanes), BF),
                pltpu.VMEM((chunks, rows, lanes), BF),
                pltpu.VMEM((chunks, rows, lanes), BF),
                pltpu.VMEM((chunks, rows, 128), F32),
                pltpu.VMEM((chunks, rows, lanes), F32),
                pltpu.VMEM((chunks, rows, lanes), F32),
                pltpu.VMEM((lanes, rows), F32),
            ],
        ),
        compiler_params=pltpu.CompilerParams(vmem_limit_bytes=VMEM_LIMIT),
        cost_estimate=pl.CostEstimate(
            flops=pairs * rows * rows * 640,
            bytes_accessed=chunks * rows * width * 8,
            transcendentals=pairs * rows * rows,
        ),
    )(overlap, qkv_own, qkv_other, ids, flat, totals, *grads)


def layer_norm_forward(hidden, norm_gain, norm_shift):
    centered_input = hidden - jnp.mean(hidden, -1, keepdims=True)
    inverse_deviation = lax.rsqrt(
        jnp.mean(centered_input * centered_input, -1, keepdims=True) + NORM_EPS
    )
    standardized_input = centered_input * inverse_deviation
    return (standardized_input * norm_gain + norm_shift, standardized_input, inverse_deviation)


def layer_norm_backward(upstream_gradient, standardized_input, inverse_deviation, norm_gain):
    scaled_rows = upstream_gradient * norm_gain
    centered_input = (
        scaled_rows
        - jnp.mean(scaled_rows, -1, keepdims=True)
        - standardized_input * jnp.mean(scaled_rows * standardized_input, -1, keepdims=True)
    )
    return (
        inverse_deviation * centered_input,
        jnp.sum(upstream_gradient * standardized_input, 0),
        jnp.sum(upstream_gradient, 0),
    )


def send(value, perm):
    return lax.ppermute(value, AXES, perm)


def gather_stages(block, perms):
    for perm in perms[:-1]:
        block = jnp.concatenate([block, send(block, perm)], axis=0)
    return [block, send(block, perms[-1])]


def scatter_stages(keep, away, perms):
    for perm in perms[:0:-1]:
        arrived = send(away, perm).astype(F32)
        half = keep.shape[0] // 2
        keep = keep.astype(F32)
        away = (keep[half:] + arrived[half:]).astype(BF)
        keep = keep[:half] + arrived[:half]
        keep = keep.astype(BF)
    return keep.astype(F32) + send(away, perms[0]).astype(F32)


def pieces(count, rows, columns):
    return jax.ShapeDtypeStruct((count, rows, columns), BF)


def body(
    plan,
    tokens,
    segment_ids,
    w_query,
    b_query,
    w_key,
    w_value,
    b_value,
    w_out,
    b_out,
    g_attn,
    n_attn,
    w_in,
    b_in,
    w_back,
    b_back,
    g_ffn,
    n_ffn,
    cotangent,
):
    chips, groups, heads, ctx = plan.chips, plan.groups, plan.heads, plan.ctx
    core = lax.axis_index("dp")
    place = lax.axis_index("ctx")
    device = (core * ctx + place) * plan.fsdp + lax.axis_index("fsdp")
    side, group = place // groups, place % groups
    rows = tokens.shape[1]
    shard = w_query.shape[0]
    hidden = w_back.shape[0]
    part = hidden // 2
    lanes = heads * HD
    half_d = D // 2
    width = 3 * lanes
    vectors = (b_query, b_value, b_out, g_attn, n_attn, b_back, g_ffn, n_ffn)
    extra_size = len(vectors) * shard + hidden + rows
    extra_rows = 16 * (-(-extra_size // (16 * width)))
    swap = plan.core_swap()

    def lookup(table):
        return lax.dynamic_index_in_dim(jnp.asarray(table), device, 0, False)

    def mine(columns, size, axis=1):
        return lax.dynamic_slice_in_dim(columns, core * size, size, axis)

    inputs = tokens[0]
    block = send(inputs, plan.turn())[None]
    for perm in plan.group_perms():
        block = jnp.concatenate([block, send(block, perm)], axis=0)
    tokens_own = block
    tokens_other = send(tokens_own, swap)

    extra = jnp.concatenate(list(vectors) + [b_in, segment_ids[0].astype(BF)])
    extra = jnp.pad(extra, (0, extra_rows * width - extra_size)).reshape(extra_rows, width)
    heads_in = jnp.stack(
        [mine(w, half_d).reshape(shard, groups, lanes) for w in (w_query, w_key, w_value)], axis=2
    ).reshape(shard, groups, width)

    def message(d):
        columns = lax.dynamic_index_in_dim(heads_in, group ^ d, 1, False)
        return jnp.concatenate([columns, extra], axis=0)

    arrived = [message(0)] + [
        send(message(d), plan.group_direct(d)) for d in range(1, groups)
    ]
    gathered = gather_stages(jnp.stack(arrived), plan.side_perms())
    side_table = plan.side_pieces()
    heads_mat, extras = route(
        gathered,
        lookup(invert(side_table)),
        [pieces(chips, shard, width), pieces(chips, extra_rows, width)],
        [((0, 1), i, 0, shard, 0, i, 0) for i in range(chips)]
        + [((0, 1), i, shard, extra_rows, 1, i, 0) for i in range(chips)],
    )
    heads_mat = heads_mat.reshape(D, width)
    extras = extras.reshape(chips, -1)

    def vector(which):
        return extras[:, which * shard : (which + 1) * shard].reshape(-1)

    query_bias, value_bias, out_bias, gain_one, shift_one, back_bias, gain_two, shift_two = [
        vector(which) for which in range(len(vectors))
    ]
    at = len(vectors) * shard
    in_bias = lax.dynamic_index_in_dim(
        extras[:, at : at + hidden].reshape(chips, 2, part), core, 1, False
    ).reshape(-1)
    ids_here = lax.dynamic_index_in_dim(
        extras[:, at + hidden : at + hidden + rows].reshape(ctx, plan.fsdp, rows),
        lax.axis_index("fsdp"),
        1,
        False,
    )
    ids_there = send(ids_here, swap)
    ids_all = jnp.where(core == side, ids_here, ids_there).astype(F32)
    chunk_table = plan.table(lambda c, j, f: [plan.chunk_of(c, j, p) for p in range(ctx)])
    chosen = lookup(chunk_table)[:, None] == jnp.arange(ctx)[None]
    ids = jnp.sum(jnp.where(chosen[:, :, None], ids_all[None], 0.0), axis=1)
    first, last = ids[:, 0], ids[:, -1]
    overlap = ((first[:, None] <= last[None]) & (first[None] <= last[:, None])).astype(jnp.int32)
    ids = ids[:, None, :]

    perms = plan.chip_perms()
    out_parts = gather_stages(mine(w_out, half_d)[None], perms)
    w_in_mine = lax.dynamic_index_in_dim(
        w_in.reshape(shard, chips, 2, part), core, 2, False
    ).reshape(shard, chips * part)
    in_parts = gather_stages(w_in_mine[None], perms)
    back_parts = gather_stages(mine(w_back, part, 0)[None], perms)
    chip_gather = plan.chip_gather()
    out_table = plan.out_rows(shard)
    out_gather = np.take_along_axis(chip_gather, out_table, axis=1)

    def placed(parts, table):
        _, piece_rows, columns = parts[0].shape
        (result,) = route(
            parts,
            lookup(table),
            [pieces(chips, piece_rows, columns)],
            [((0, 1), i, 0, piece_rows, 0, i, 0) for i in range(chips)],
        )
        return result.reshape(chips * piece_rows, columns)

    out_mine = placed(out_parts, out_gather)
    out_there = send(out_mine, swap)
    out_mat = jnp.where(
        core == 0,
        jnp.concatenate([out_mine, out_there], axis=1),
        jnp.concatenate([out_there, out_mine], axis=1),
    )
    in_mat = placed(in_parts, chip_gather)
    back_mat = placed(back_parts, chip_gather)

    start = core * half_d + group * lanes
    zero_bias = jnp.zeros((lanes,), BF)
    heads_bias = jnp.concatenate(
        [
            lax.dynamic_slice_in_dim(query_bias, start, lanes),
            zero_bias,
            lax.dynamic_slice_in_dim(value_bias, start, lanes),
        ]
    ).astype(F32)

    def project(block):
        return (
            jnp.einsum("ptd,dw->ptw", block, heads_mat, preferred_element_type=F32) + heads_bias
        ).astype(BF)

    qkv_own, qkv_other = project(tokens_own), project(tokens_other)
    *sent, flat, totals = attend_forward(qkv_own, qkv_other, ids, overlap, heads)
    attended = jnp.concatenate([send(sent[p], plan.outward(p)) for p in range(ctx)], axis=1)

    branch = nn(attended, out_mat) + out_bias
    normed, standard_one, inverse_one = layer_norm_forward(
        inputs.astype(F32) + branch, gain_one, shift_one
    )
    low_own = normed.astype(BF)
    low_other = send(low_own, swap)

    def feed(low):
        inner = nn(low, in_mat) + in_bias
        cdf = 0.5 * (1.0 + lax.erf(inner * (0.5**0.5)))
        slope = cdf + inner * (jnp.exp(-0.5 * inner * inner) * (1.0 / (2.0 * np.pi) ** 0.5))
        return (inner * cdf).astype(BF), slope

    active_own, slope_own = feed(low_own)
    active_other, slope_other = feed(low_other)
    fed = nn(active_own, back_mat) + send(nn(active_other, back_mat), swap) + back_bias
    result, standard_two, inverse_two = layer_norm_forward(normed + fed, gain_two, shift_two)
    grad_sum_two, grad_gain_two, grad_shift_two = layer_norm_backward(
        cotangent[0].astype(F32), standard_two, inverse_two, gain_two
    )
    up_own = grad_sum_two.astype(BF)
    up_other = send(up_own, swap)
    grad_back_bias = jnp.sum(up_own.astype(F32), 0)

    grad_inner_own = (nt(up_own, back_mat) * slope_own).astype(BF)
    grad_inner_other = (nt(up_other, back_mat) * slope_other).astype(BF)
    chip_spread = plan.chip_spread()

    def spread(grad, table, piece_rows):
        columns = grad.shape[1]
        keep, away = route(
            [grad.astype(BF).reshape(chips, piece_rows, columns)],
            lookup(table),
            [pieces(chips // 2, piece_rows, columns)] * 2,
            [
                ((0,), k, 0, piece_rows, k // (chips // 2), k % (chips // 2), 0)
                for k in range(chips)
            ],
        )
        return scatter_stages(keep, away, perms)[0]

    grad_back_mat = spread(
        tn(active_own, up_own) + tn(active_other, up_other), chip_spread, part
    )
    grad_in_mat = spread(
        tn(low_own, grad_inner_own) + tn(low_other, grad_inner_other), chip_spread, shard
    )
    grad_in_bias = jnp.sum(grad_inner_own.astype(F32), 0) + jnp.sum(
        grad_inner_other.astype(F32), 0
    )
    grad_normed = (
        grad_sum_two + nt(grad_inner_own, in_mat) + send(nt(grad_inner_other, in_mat), swap)
    )
    grad_sum_one, grad_gain_one, grad_shift_one = layer_norm_backward(
        grad_normed, standard_one, inverse_one, gain_one
    )
    grad_branch = grad_sum_one.astype(BF)
    grad_out_bias = jnp.sum(grad_branch.astype(F32), 0)
    grad_attended = nt(grad_branch, out_mat).astype(BF)
    grads = [
        send(grad_attended[:, p * lanes : (p + 1) * lanes], plan.inward(p)) for p in range(ctx)
    ]
    grad_out_mine = tn(attended, mine(grad_branch, half_d))
    grad_out_there = tn(
        attended, lax.dynamic_slice_in_dim(grad_branch, (1 - core) * half_d, half_d, 1)
    )
    grad_out = grad_out_mine + send(grad_out_there.astype(BF), swap).astype(F32)
    out_spread = np.take_along_axis(invert(out_table), chip_spread, axis=1)
    grad_out_mat = spread(grad_out, out_spread, shard)

    down_own, down_other = attend_backward(
        qkv_own, qkv_other, ids, overlap, grads, flat, totals, heads
    )

    def back_project(down):
        return jnp.einsum("ptw,dw->ptd", down, heads_mat, preferred_element_type=F32)

    towards = send(back_project(down_other).astype(BF), swap)
    block = (back_project(down_own) + towards.astype(F32)).astype(BF)
    for perm in plan.group_perms()[::-1]:
        half = block.shape[0] // 2
        block = (block[:half].astype(F32) + send(block[half:], perm).astype(F32)).astype(BF)
    grad_inputs = grad_sum_one + send(block[0], plan.turn()).astype(F32)

    grad_heads = jnp.einsum(
        "ptd,ptw->dw", tokens_own, down_own, preferred_element_type=F32
    ) + jnp.einsum("ptd,ptw->dw", tokens_other, down_other, preferred_element_type=F32)
    grad_heads_bias = jnp.sum(down_own.astype(F32), (0, 1)) + jnp.sum(
        down_other.astype(F32), (0, 1)
    )

    def whole_bias(columns):
        return lax.dynamic_update_slice_in_dim(jnp.zeros((D,), F32), columns, start, 0)

    grad_vectors = (
        whole_bias(grad_heads_bias[:lanes]),
        whole_bias(grad_heads_bias[2 * lanes :]),
        grad_out_bias,
        grad_gain_one,
        grad_shift_one,
        grad_back_bias,
        grad_gain_two,
        grad_shift_two,
    )
    in_pairs = grad_in_bias.reshape(chips, 1, part) * (
        jnp.arange(2)[None, :, None] == core
    ).astype(F32)
    grad_extra = jnp.concatenate(
        [grad.reshape(chips, shard) for grad in grad_vectors]
        + [in_pairs.reshape(chips, hidden)],
        axis=1,
    )
    grad_extra = jnp.pad(
        grad_extra, ((0, 0), (0, extra_rows * width - grad_extra.shape[1]))
    ).reshape(chips, extra_rows, width)
    keep, away = route(
        [grad_heads.astype(BF).reshape(chips, shard, width), grad_extra.astype(BF)],
        lookup(side_table),
        [pieces(chips // 2, shard + extra_rows, width)] * 2,
        [
            ((which,), k, 0, size, k // (chips // 2), k % (chips // 2), which * shard)
            for which, size in ((0, shard), (1, extra_rows))
            for k in range(chips)
        ],
    )
    mine_by_group = scatter_stages(keep, away, plan.side_perms())
    low_by_group = mine_by_group.astype(BF)
    by_group = [low_by_group[0]] + [
        send(low_by_group[d], plan.group_direct(d)) for d in range(1, groups)
    ]
    by_group = jnp.stack(by_group).astype(F32)
    grad_extras = jnp.sum(by_group[:, shard:], 0)
    grad_columns = jnp.stack(
        [lax.dynamic_index_in_dim(by_group, group ^ d, 0, False)[:shard] for d in range(groups)]
    )
    grad_columns = grad_columns.reshape(groups, shard, 3, lanes).transpose(2, 1, 0, 3)
    grad_columns = grad_columns.reshape(3, shard, half_d)

    def both(half, axis):
        there = send(half, swap)
        return jnp.where(
            core == 0, jnp.stack([half, there], axis=axis), jnp.stack([there, half], axis=axis)
        )

    grad_columns = both(grad_columns, 2).reshape(3, shard, D)
    grad_out_mat = both(grad_out_mat, 1).reshape(shard, D)
    grad_in_mat = both(grad_in_mat.reshape(shard, chips, part), 2).reshape(shard, FF)
    grad_back_mat = both(grad_back_mat, 0).reshape(hidden, D)
    sums = (grad_extras + send(grad_extras, swap)).reshape(-1)
    small = [sums[which * shard : (which + 1) * shard] for which in range(len(vectors))]
    return (
        result.astype(BF)[None],
        grad_inputs[None],
        grad_columns[0],
        small[0],
        grad_columns[1],
        grad_columns[2],
        small[1],
        grad_out_mat,
        small[2],
        small[3],
        small[4],
        grad_in_mat,
        sums[at : at + hidden],
        grad_back_mat,
        small[5],
        small[6],
        small[7],
    )


def solution(mesh):
    owned = ("ctx", "fsdp")
    matrix, vector = P(owned, None), P(owned)
    sequence = P(("dp", "fsdp"), "ctx", None)
    return jax.shard_map(
        partial(body, Plan(mesh)),
        mesh=mesh,
        in_specs=(
            sequence,
            P(("dp", "fsdp"), "ctx"),
            matrix,
            vector,
            matrix,
            matrix,
            vector,
            matrix,
            vector,
            vector,
            vector,
            matrix,
            vector,
            matrix,
            vector,
            vector,
            vector,
            sequence,
        ),
        out_specs=(
            sequence,
            sequence,
            matrix,
            vector,
            matrix,
            matrix,
            vector,
            matrix,
            vector,
            vector,
            vector,
            matrix,
            vector,
            matrix,
            vector,
            vector,
            vector,
        ),
        check_vma=False,
    )
```

time: 2170 us -> 507 us (0.23)
  waiting for transfers between devices: 1610 us -> 171 us
  blocking collectives: 216 us -> 0 us
  matrix products: 175 us -> 62.3 us
  starting transfers between devices: 0.85 us -> 95.6 us
  Pallas kernels: 0 us -> 91.4 us
  local copies, waits for them, and re-layouts: 106 us -> 43.5 us
    reduce_scatter x5 -> x0, waiting for transfers between devices: 951 us -> none  [the longest x1 352 us: body(): lax.psum_scatter(local_grads[11], ('ctx', 'fsdp'), scatter_dimension=0, t...]
    all_gather x8 -> x0, waiting for transfers between devices: 400 us -> none  [the longest x1 112 us: body(): lax.all_gather(shards[9], ('ctx', 'fsdp'), axis=0, tiled=True)]
    unnamed x20 -> x0, waiting for transfers between devices: 262 us -> none
    ppermute x0 -> x70, waiting for transfers between devices: none -> 171 us  [send(): return lax.ppermute(value, AXES, perm)]
    unnamed x2 -> x0, blocking collectives: 158 us -> none
    dot_general x74 -> x22, matrix products: 175 us -> 62.3 us  [the longest x6 23.1 us: tn(): lax.dot_general(left, right, (((0,), (0,)), ((), ())), preferred_element_...]
    ppermute x0 -> x70, starting transfers between devices: none -> 95.6 us  [send(): return lax.ppermute(value, AXES, perm)]
    pallas_call x0 -> x10, Pallas kernels: none -> 91.4 us  [the longest x1 32.9 us: attend_backward(): pl.pallas_call(kernel, out_shape=[jax.ShapeDtypeStruct((half, rows, width...]
  transfers between devices with their start and end apart: 17 -> 70, of which waited for: 15 -> 23; matrix products, arithmetic and copies ran while one was open for 7% -> 21% of each run, Pallas kernels for 0% -> 18%
where the time goes in v1:
time: 507 us; the launch traced here: 503 us
  waiting for transfers between devices  171 us (34%)
  starting transfers between devices  95.6 us (19%)
  Pallas kernels  91.4 us (18%)
  matrix products  62.3 us (12%)
  local copies, waits for them, and re-layouts  43.5 us (9%)
  other arithmetic  36.1 us (7%)
    ppermute x70, waiting for transfers between devices, send(): return lax.ppermute(value, AXES, perm)  171 us
    ppermute x70, starting transfers between devices, send(): return lax.ppermute(value, AXES, perm)  95.6 us
    pallas_call x1, Pallas kernels, attend_backward(): pl.pallas_call(kernel, out_shape=[jax.ShapeDtypeStruct((half, rows, width...  32.9 us
    pallas_call x1, Pallas kernels, attend_forward(): pl.pallas_call(kernel, out_shape=[jax.ShapeDtypeStruct((rows, lanes), BF)...  32.5 us
    pallas_call x8, Pallas kernels, route(): pl.pallas_call(kernel, out_shape=outs, in_specs=[pl.BlockSpec(memory_spac...  25.9 us
    dot_general x6, matrix products, tn(): lax.dot_general(left, right, (((0,), (0,)), ((), ())), preferred_element_...  23.1 us
    unnamed x132, local copies, waits for them, and re-layouts  13.1 us
    dot_general x5, matrix products, nn(): lax.dot_general(left, right, (((1,), (0,)), ((), ())), preferred_element_...  12.2 us
  transfers between devices with their start and end apart: 70, of which 23 were waited for; matrix products, arithmetic and copies ran while one was open for 21% of the time, Pallas kernels for 18%

profile of v1, /device:TPU:0, one launch (start us, length us, event | category | flops | bytes accessed | tf_op | source)
XLA Modules:
  0.0 502.8 jit_solution(6802067287246291738)
XLA Ops:
  1.5 6.1 %concatenate.80 = bf16[1024]{0:T(1024)(128)(2,1)S(1)} concatenate(bf16[64]{0:T(256)(128)(2,1)} %param.28, bf16[64]{0:T(256)(128)(2,1)} %param.31, bf16[64]{0:T(256)(128)(2,1)} %param.33, bf16[64]{0:T(256)(128)(2,1)} %param.34, bf16[64]{0:T(256)(128)(2,1)} %param.35, bf16[64]{0:T(256)(128)(2,1)} %param.39, bf16[64]{0:T(256)(128)(2,1)} %param.40, bf16[64]{0:T(256)(128)(2,1)} %param.41, ...), dimensions={0} | concatenate | bytes 4096 | tf_op jit(solution)/shard_map/concatenate | solution.py:513
  10.1 3.0 collective-permute-start
  16.7 2.0 collective-permute-start.23
  23.4 2.0 collective-permute-start.27
  28.3 12.1 %collective-permute-start.19 = (bf16[2,64,512]{2,1,0:T(8,128)(2,1)S(1)}, bf16[2,64,512]{2,1,0:T(8,128)(2,1)S(1)}, u32[]{:S(2)}, u32[]{:S(2)}) collective-permute-start(bf16[2,64,512]{2,1,0:T(8,128)(2,1)S(1)} %pad_maximum_fusion.11), channel_id=1, source_target_pairs={{0,8},{1,9},{2,10},{3,11},{4,12},{5,13},{6,14},{7,15},{8,0},{9,1},... | collective-permute-start | bytes 393224 | tf_op jit(solution)/shard_map/ppermute | solution.py:438
  40.4 5.9 %collective-permute-done.19 = bf16[2,64,512]{2,1,0:T(8,128)(2,1)S(1)} collective-permute-done((bf16[2,64,512]{2,1,0:T(8,128)(2,1)S(1)}, bf16[2,64,512]{2,1,0:T(8,128)(2,1)S(1)}, u32[]{:S(2)}, u32[]{:S(2)}) %collective-permute-start.19) | collective-permute-done | bytes 131104 | tf_op jit(solution)/shard_map/ppermute | solution.py:438
  50.8 2.3 collective-permute-start.24
  54.6 2.3 collective-permute-start.4
  57.6 36.7 %collective-permute-done.24 = bf16[2,64,2048]{2,1,0:T(8,128)(2,1)S(1)} collective-permute-done((bf16[2,64,2048]{2,1,0:T(8,128)(2,1)S(1)}, bf16[2,64,2048]{2,1,0:T(8,128)(2,1)S(1)}, u32[]{:S(2)}, u32[]{:S(2)}) %collective-permute-start.24) | collective-permute-done | bytes 524320 | tf_op jit(solution)/shard_map/ppermute | solution.py:438
  96.9 6.8 %collective-permute-done.28 = bf16[2,128,1024]{2,1,0:T(8,128)(2,1)S(1)} collective-permute-done((bf16[2,128,1024]{2,1,0:T(8,128)(2,1)S(1)}, bf16[2,128,1024]{2,1,0:T(8,128)(2,1)S(1)}, u32[]{:S(2)}, u32[]{:S(2)}) %collective-permute-start.28) | collective-permute-done | bytes 524320 | tf_op jit(solution)/shard_map/ppermute | solution.py:438
  109.0 2.6 shard_map.368
  114.7 2.3 shard_map.370
  117.4 2.4 constant_dynamic-update-slice_fusion.13.refs_0_
  121.7 3.1 add_convert_fusion.5.other_ref
  124.9 32.5 %shard_map.369 = (bf16[256,128]{1,0:T(8,128)(2,1)S(1)}, bf16[256,128]{1,0:T(8,128)(2,1)S(1)}, bf16[256,128]{1,0:T(8,128)(2,1)S(1)}, bf16[256,128]{1,0:T(8,128)(2...) custom-call(s32[8,8]{1,0:T(8,128)S(1)} %and_convert_fusion.overlap_r, ...), custom_call_target="tpu_custom_call" | custom-call | flops 2147483648 | bytes 3145728 | tf_op jit(solution)/shard_map/pallas_call | solution.py:267
  162.7 2.8 collective-permute-done.11
  166.4 22.3 %collective-permute-done.12 = bf16[256,128]{1,0:T(8,128)(2,1)S(1)} collective-permute-done((bf16[256,128]{1,0:T(8,128)(2,1)S(1)}, bf16[256,128]{1,0:T(8,128)(2,1)S(1)}, u32[]{:S(2)}, u32[]{:S(2)}) %collective-permute-start.12) | collective-permute-done | bytes 65568 | tf_op jit(solution)/shard_map/ppermute | solution.py:438
  188.7 12.5 %collective-permute-start.15 = (bf16[256,128]{1,0:T(8,128)(2,1)S(1)}, bf16[256,128]{1,0:T(8,128)(2,1)S(1)}, u32[]{:S(2)}, u32[]{:S(2)}) collective-permute-start(bf16[256,128]{1,0:T(8,128)(2,1)S(1)} %get-tuple-element.46), channel_id=1, source_target_pairs={{0,10},{1,11},{2,8},{3,9},{4,14},{5,15},{6,12},{7,13},{8,26},{9,27... | collective-permute-start | bytes 196616 | tf_op jit(solution)/shard_map/ppermute | solution.py:438
  201.3 3.5 collective-permute-done.15
  204.9 2.6 collective-permute-start.17
  207.6 1.9 collective-permute-done.17
  212.0 3.4 collective-permute-start.31
  216.1 4.8 shard_map.371
  221.0 4.6 shard_map.372
  225.6 2.5 convolution_add_fusion
  231.4 3.7 convolution_add_fusion.1
  235.3 3.7 fusion.83
  242.3 3.8 convert_reduce_fusion.1
  246.3 3.1 fusion.71
  249.9 3.3 convert_reduce_fusion
  254.8 5.7 %fusion.85 = f32[1024,2048]{1,0:T(8,128)} fusion(bf16[256,1024]{1,0:T(8,128)(2,1)} %fusion.32, bf16[256,2048]{1,0:T(8,128)(2,1)S(1)} %copy-done.47), kind=kOutput, calls=%fused_computation.245 | convolution fusion | flops 1073741824 | bytes 9961472 | tf_op jit(solution)/shard_map/dot_general | solution.py:200
  260.5 4.1 add_convert_fusion
  268.9 3.4 collective-permute-start.41
  273.0 2.0 collective-permute-start.38
  279.8 2.8 shard_map.377
  288.1 32.9 %shard_map.373 = (bf16[4,256,384]{2,1,0:T(8,128)(2,1)S(1)}, bf16[4,256,384]{2,1,0:T(8,128)(2,1)S(1)}) custom-call(s32[8,8]{1,0:T(8,128)S(1)} %and_convert_fusion.overlap_ref, bf16[4,256,384]{2,1,0:T(8,128)(2,1)S(1)} %copy-done.11, bf16[4,256,384]{2,1,0:T(8,128)(2,1)S(1)} %copy-done.9, f32[8,1,256]{2,1,0:T(1,128)S(1)} %broadcast_in_dim.39.ids_ref, ...), custom_call_target="tpu_custom_call" | custom-call | flops 5368709120 | bytes 6291456 | tf_op jit(solution)/shard_map/pallas_call | solution.py:378
  322.7 2.9 fusion.70
  325.6 3.0 fusion.14
  328.6 2.4 shard_map.374
  331.0 6.4 %collective-permute-start.47 = (bf16[8,80,384]{2,1,0:T(8,128)(2,1)S(1)}, bf16[8,80,384]{2,1,0:T(8,128)(2,1)S(1)}, u32[]{:S(2)}, u32[]{:S(2)}) collective-permute-start(bf16[8,80,384]{2,1,0:T(8,128)(2,1)S(1)} %get-tuple-element.54), channel_id=1, source_target_pairs={{0,8},{1,9},{2,10},{3,11},{4,12},{5,13},{6,14},{7,15},{8,0},{9,1},... | collective-permute-start | bytes 1474568 | tf_op jit(solution)/shard_map/ppermute | solution.py:438
  337.4 7.0 %add_convert_fusion.1 = bf16[1024,2048]{1,0:T(8,128)(2,1)} fusion(f32[1024,2048]{1,0:T(8,128)} %fusion.85, bf16[256,1024]{1,0:T(8,128)(2,1)} %collective-permute-done.31, bf16[256,2048]{1,0:T(8,128)(2,1)S(1)} %copy-done.46), kind=kOutput, calls=%fused_computation.1 | convolution fusion | flops 1077936128 | bytes 14155776 | tf_op jit(solution)/shard_map/dot_general | solution.py:200
  344.4 4.1 shard_map.376
  351.7 6.2 %collective-permute-done.48 = bf16[4,80,384]{2,1,0:T(8,128)(2,1)S(1)} collective-permute-done((bf16[4,80,384]{2,1,0:T(8,128)(2,1)S(1)}, bf16[4,80,384]{2,1,0:T(8,128)(2,1)S(1)}, u32[]{:S(2)}, u32[]{:S(2)}) %collective-permute-start.48) | collective-permute-done | bytes 245792 | tf_op jit(solution)/shard_map/ppermute | solution.py:438
  358.8 2.5 convert_element_type.458
  361.3 2.6 convert_element_type.443
  363.9 3.3 collective-permute-start.50
  367.3 2.7 convolution_convert_fusion
  370.1 7.4 %collective-permute-done.49 = bf16[80,384]{1,0:T(8,128)(2,1)S(1)} collective-permute-done((bf16[80,384]{1,0:T(8,128)(2,1)S(1)}, bf16[80,384]{1,0:T(8,128)(2,1)S(1)}, u32[]{:S(2)}, u32[]{:S(2)}) %collective-permute-start.49) | collective-permute-done | bytes 61472 | tf_op jit(solution)/shard_map/ppermute | solution.py:438
  383.3 2.3 shard_map.375
  390.8 2.2 convert_element_type.459
  395.8 2.1 convert_element_type.444
  403.3 9.3 %collective-permute-done.56 = bf16[4,64,512]{2,1,0:T(8,128)(2,1)S(1)} collective-permute-done((bf16[4,64,512]{2,1,0:T(8,128)(2,1)S(1)}, bf16[4,64,512]{2,1,0:T(8,128)(2,1)S(1)}, u32[]{:S(2)}, u32[]{:S(2)}) %collective-permute-start.56) | collective-permute-done | bytes 262176 | tf_op jit(solution)/shard_map/ppermute | solution.py:438
  412.9 6.6 %collective-permute-done.57 = bf16[2,64,512]{2,1,0:T(8,128)(2,1)S(1)} collective-permute-done((bf16[2,64,512]{2,1,0:T(8,128)(2,1)S(1)}, bf16[2,64,512]{2,1,0:T(8,128)(2,1)S(1)}, u32[]{:S(2)}, u32[]{:S(2)}) %collective-permute-start.57) | collective-permute-done | bytes 131104 | tf_op jit(solution)/shard_map/ppermute | solution.py:438
  420.5 3.3 collective-permute-done.61
  424.4 2.9 add_convert_fusion.2
  428.2 30.3 %collective-permute-done.67 = bf16[2,128,1024]{2,1,0:T(8,128)(2,1)S(1)} collective-permute-done((bf16[2,128,1024]{2,1,0:T(8,128)(2,1)S(1)}, bf16[2,128,1024]{2,1,0:T(8,128)(2,1)S(1)}, u32[]{:S(2)}, u32[]{:S(2)}) %collective-permute-start.67) | collective-permute-done | bytes 524320 | tf_op jit(solution)/shard_map/ppermute | solution.py:438
  458.8 9.8 %collective-permute-done.62 = bf16[2,64,2048]{2,1,0:T(8,128)(2,1)S(1)} collective-permute-done((bf16[2,64,2048]{2,1,0:T(8,128)(2,1)S(1)}, bf16[2,64,2048]{2,1,0:T(8,128)(2,1)S(1)}, u32[]{:S(2)}, u32[]{:S(2)}) %collective-permute-start.62) | collective-permute-done | bytes 524320 | tf_op jit(solution)/shard_map/ppermute | solution.py:438
  469.3 2.1 collective-permute-start.45
  471.4 2.8 collective-permute-done.68
  474.4 5.3 %collective-permute-done.63 = bf16[1,64,2048]{2,1,0:T(8,128)(2,1)S(1)} collective-permute-done((bf16[1,64,2048]{2,1,0:T(8,128)(2,1)S(1)}, bf16[1,64,2048]{2,1,0:T(8,128)(2,1)S(1)}, u32[]{:S(2)}, u32[]{:S(2)}) %collective-permute-start.63) | collective-permute-done | bytes 262176 | tf_op jit(solution)/shard_map/ppermute | solution.py:438
  480.0 5.3 %collective-permute-done.45 = bf16[1,256,1024]{2,1,0:T(8,128)(2,1)S(1)} collective-permute-done((bf16[1,256,1024]{2,1,0:T(8,128)(2,1)S(1)}, bf16[1,256,1024]{2,1,0:T(8,128)(2,1)S(1)}, u32[]{:S(2)}, u32[]{:S(2)}) %collective-permute-start.45) | collective-permute-done | bytes 524320 | tf_op jit(solution)/shard_map/ppermute | solution.py:438
  486.3 5.3 %collective-permute-start.46 = (bf16[256,1024]{1,0:T(8,128)(2,1)}, bf16[256,1024]{1,0:T(8,128)(2,1)}, u32[]{:S(2)}, u32[]{:S(2)}) collective-permute-start(bf16[256,1024]{1,0:T(8,128)(2,1)} %fusion.34), channel_id=1, source_target_pairs={{0,0},{1,1},{2,2},{3,3},{4,4},{5,5},{6,6},{7,7},{8,16},{9,17},{10,... | collective-permute-start | bytes 1572872 | tf_op jit(solution)/shard_map/ppermute | solution.py:438
  498.1 2.3 maximum_select_fusion.2
  500.5 2.1 add_bitcast_fusion
  (406 shorter events, 103.8 us)
Async XLA Ops:
  10.1 13.3 %collective-permute-start = (bf16[80,384]{1,0:T(8,128)(2,1)S(1)}, bf16[80,384]{1,0:T(8,128)(2,1)S(1)}, u32[]{:S(2)}, u32[]{:S(2)}) collective-permute-start(bf16[80,384]{1,0:T(8,128)(2,1)S(1)} %get-tuple-element.132), channel_id=1, source_target_pairs={{0,2},{1,3},{2,0},{3,1},{4,6},{5,7},{6,4},{7,5},{8,10},{9,11},{10,... | collective-permute-start | bytes 184328 | tf_op jit(solution)/shard_map/ppermute | solution.py:438
  13.1 10.3 %collective-permute-start.1 = (bf16[80,384]{1,0:T(8,128)(2,1)S(1)}, bf16[80,384]{1,0:T(8,128)(2,1)S(1)}, u32[]{:S(2)}, u32[]{:S(2)}) collective-permute-start(bf16[80,384]{1,0:T(8,128)(2,1)S(1)} %get-tuple-element.133), channel_id=1, source_target_pairs={{0,4},{1,5},{2,6},{3,7},{4,0},{5,1},{6,2},{7,3},{8,12},{9,13},{10,... | collective-permute-start | bytes 184328 | tf_op jit(solution)/shard_map/ppermute | solution.py:438
  14.7 10.7 %collective-permute-start.2 = (bf16[80,384]{1,0:T(8,128)(2,1)S(1)}, bf16[80,384]{1,0:T(8,128)(2,1)S(1)}, u32[]{:S(2)}, u32[]{:S(2)}) collective-permute-start(bf16[80,384]{1,0:T(8,128)(2,1)S(1)} %get-tuple-element.134), channel_id=1, source_target_pairs={{0,6},{1,7},{2,4},{3,5},{4,2},{5,3},{6,0},{7,1},{8,14},{9,15},{10,... | collective-permute-start | bytes 184328 | tf_op jit(solution)/shard_map/ppermute | solution.py:438
  16.7 34.0 %collective-permute-start.23 = (bf16[1,64,2048]{2,1,0:T(8,128)(2,1)S(1)}, bf16[1,64,2048]{2,1,0:T(8,128)(2,1)S(1)}, u32[]{:S(2)}, u32[]{:S(2)}) collective-permute-start(bf16[1,64,2048]{2,1,0:T(8,128)(2,1)S(1)} %broadcast_in_dim_reshape.3), channel_id=1, source_target_pairs={{0,4},{1,5},{2,6},{3,7},{4,0},{5,1},{6,2},{7,3},{8,12},{9,13},{10,... | collective-permute-start | bytes 786440 | tf_op jit(solution)/shard_map/ppermute | solution.py:438
  18.7 8.3 %collective-permute-start.6 = (bf16[256,1024]{1,0:T(8,128)(2,1)}, bf16[256,1024]{1,0:T(8,128)(2,1)S(1)}, u32[]{:S(2)}, u32[]{:S(2)}) collective-permute-start(bf16[256,1024]{1,0:T(8,128)(2,1)} %bitcast.222), channel_id=1, source_target_pairs={{0,0},{1,1},{2,2},{3,3},{4,4},{5,5},{6,6},{7,7},{8,16},{9,17},{10,... | collective-permute-start | bytes 1572872 | tf_op jit(solution)/shard_map/ppermute | solution.py:438
  23.4 29.7 %collective-permute-start.27 = (bf16[1,128,1024]{2,1,0:T(8,128)(2,1)S(1)}, bf16[1,128,1024]{2,1,0:T(8,128)(2,1)S(1)}, u32[]{:S(2)}, u32[]{:S(2)}) collective-permute-start(bf16[1,128,1024]{2,1,0:T(8,128)(2,1)S(1)} %dynamic-slice_bitcast_fusion), channel_id=1, source_target_pairs={{0,4},{1,5},{2,6},{3,7},{4,0},{5,1},{6,2},{7,3},{8,12},{9,13},{10,... | collective-permute-start | bytes 786440 | tf_op jit(solution)/shard_map/ppermute | solution.py:438
  25.4 29.2 %collective-permute-start.3 = (bf16[4,80,384]{2,1,0:T(8,128)(2,1)S(1)}, bf16[4,80,384]{2,1,0:T(8,128)(2,1)S(1)}, u32[]{:S(2)}, u32[]{:S(2)}) collective-permute-start(bf16[4,80,384]{2,1,0:T(8,128)(2,1)S(1)} %pad_maximum_fusion.9), channel_id=1, source_target_pairs={{0,1},{1,0},{2,3},{3,2},{4,5},{5,4},{6,7},{7,6},{8,9},{9,8},{10,11... | collective-permute-start | bytes 737288 | tf_op jit(solution)/shard_map/ppermute | solution.py:438
  27.0 22.0 %collective-permute-start.7 = (bf16[1,256,1024]{2,1,0:T(8,128)(2,1)S(1)}, bf16[1,256,1024]{2,1,0:T(8,128)(2,1)S(1)}, u32[]{:S(2)}, u32[]{:S(2)}) collective-permute-start(bf16[1,256,1024]{2,1,0:T(8,128)(2,1)S(1)} %bitcast.193), channel_id=1, source_target_pairs={{0,4},{1,5},{2,6},{3,7},{4,0},{5,1},{6,2},{7,3},{8,12},{9,13},{10,... | collective-permute-start | bytes 1572872 | tf_op jit(solution)/shard_map/ppermute | solution.py:438
  28.3 17.9 %collective-permute-start.19 = (bf16[2,64,512]{2,1,0:T(8,128)(2,1)S(1)}, bf16[2,64,512]{2,1,0:T(8,128)(2,1)S(1)}, u32[]{:S(2)}, u32[]{:S(2)}) collective-permute-start(bf16[2,64,512]{2,1,0:T(8,128)(2,1)S(1)} %pad_maximum_fusion.11), channel_id=1, source_target_pairs={{0,8},{1,9},{2,10},{3,11},{4,12},{5,13},{6,14},{7,15},{8,0},{9,1},... | collective-permute-start | bytes 393224 | tf_op jit(solution)/shard_map/ppermute | solution.py:438
  46.3 10.7 %collective-permute-start.20 = (bf16[4,64,512]{2,1,0:T(8,128)(2,1)S(1)}, bf16[4,64,512]{2,1,0:T(8,128)(2,1)S(1)}, u32[]{:S(2)}, u32[]{:S(2)}) collective-permute-start(bf16[4,64,512]{2,1,0:T(8,128)(2,1)S(1)} %pad_maximum_fusion.8), channel_id=1, source_target_pairs={{0,1},{1,0},{2,3},{3,2},{4,5},{5,4},{6,7},{7,6},{8,9},{9,8},{10,11... | collective-permute-start | bytes 786440 | tf_op jit(solution)/shard_map/ppermute | solution.py:438
  49.1 57.3 %collective-permute-start.8 = (bf16[2,256,1024]{2,1,0:T(8,128)(2,1)S(1)}, bf16[2,256,1024]{2,1,0:T(8,128)(2,1)S(1)}, u32[]{:S(2)}, u32[]{:S(2)}) collective-permute-start(bf16[2,256,1024]{2,1,0:T(8,128)(2,1)S(1)} %pad_maximum_fusion.2), channel_id=1, source_target_pairs={{0,2},{1,3},{2,0},{3,1},{4,6},{5,7},{6,4},{7,5},{8,10},{9,11},{10,... | collective-permute-start | bytes 3145736 | tf_op jit(solution)/shard_map/ppermute | solution.py:438
  50.8 43.6 %collective-permute-start.24 = (bf16[2,64,2048]{2,1,0:T(8,128)(2,1)S(1)}, bf16[2,64,2048]{2,1,0:T(8,128)(2,1)S(1)}, u32[]{:S(2)}, u32[]{:S(2)}) collective-permute-start(bf16[2,64,2048]{2,1,0:T(8,128)(2,1)S(1)} %pad_maximum_fusion.6), channel_id=1, source_target_pairs={{0,8},{1,9},{2,10},{3,11},{4,12},{5,13},{6,14},{7,15},{8,0},{9,1},... | collective-permute-start | bytes 1572872 | tf_op jit(solution)/shard_map/ppermute | solution.py:438
  53.2 50.6 %collective-permute-start.28 = (bf16[2,128,1024]{2,1,0:T(8,128)(2,1)S(1)}, bf16[2,128,1024]{2,1,0:T(8,128)(2,1)S(1)}, u32[]{:S(2)}, u32[]{:S(2)}) collective-permute-start(bf16[2,128,1024]{2,1,0:T(8,128)(2,1)S(1)} %pad_maximum_fusion.7), channel_id=1, source_target_pairs={{0,8},{1,9},{2,10},{3,11},{4,12},{5,13},{6,14},{7,15},{8,0},{9,1},... | collective-permute-start | bytes 1572872 | tf_op jit(solution)/shard_map/ppermute | solution.py:438
  54.6 54.3 %collective-permute-start.4 = (bf16[8,80,384]{2,1,0:T(8,128)(2,1)S(1)}, bf16[8,80,384]{2,1,0:T(8,128)(2,1)S(1)}, u32[]{:S(2)}, u32[]{:S(2)}) collective-permute-start(bf16[8,80,384]{2,1,0:T(8,128)(2,1)S(1)} %constant_dynamic-update-slice_fusion.refs_0_), channel_id=1, source_target_pairs={{0,8},{1,9},{2,10},{3,11},{4,12},{5,13},{6,14},{7,15},{8,0},{9,1},... | collective-permute-start | bytes 1474568 | tf_op jit(solution)/shard_map/ppermute | solution.py:438
  57.0 57.6 %collective-permute-start.21 = (bf16[8,64,512]{2,1,0:T(8,128)(2,1)S(1)}, bf16[8,64,512]{2,1,0:T(8,128)(2,1)S(1)}, u32[]{:S(2)}, u32[]{:S(2)}) collective-permute-start(bf16[8,64,512]{2,1,0:T(8,128)(2,1)S(1)} %pad_maximum_fusion.5.refs_0_), channel_id=1, source_target_pairs={{0,2},{1,3},{2,0},{3,1},{4,6},{5,7},{6,4},{7,5},{8,10},{9,11},{10,... | collective-permute-start | bytes 1572872 | tf_op jit(solution)/shard_map/ppermute | solution.py:438
  95.4 22.0 %collective-permute-start.25 = (bf16[4,64,2048]{2,1,0:T(8,128)(2,1)}, bf16[4,64,2048]{2,1,0:T(8,128)(2,1)}, u32[]{:S(2)}, u32[]{:S(2)}) collective-permute-start(bf16[4,64,2048]{2,1,0:T(8,128)(2,1)} %pad_maximum_fusion.3), channel_id=1, source_target_pairs={{0,1},{1,0},{2,3},{3,2},{4,5},{5,4},{6,7},{7,6},{8,9},{9,8},{10,11... | collective-permute-start | bytes 3145736 | tf_op jit(solution)/shard_map/ppermute | solution.py:438
  104.9 53.4 %collective-permute-start.29 = (bf16[4,128,1024]{2,1,0:T(8,128)(2,1)}, bf16[4,128,1024]{2,1,0:T(8,128)(2,1)}, u32[]{:S(2)}, u32[]{:S(2)}) collective-permute-start(bf16[4,128,1024]{2,1,0:T(8,128)(2,1)} %pad_maximum_fusion.4), channel_id=1, source_target_pairs={{0,1},{1,0},{2,3},{3,2},{4,5},{5,4},{6,7},{7,6},{8,9},{9,8},{10,11... | collective-permute-start | bytes 3145736 | tf_op jit(solution)/shard_map/ppermute | solution.py:438
  108.0 13.7 %collective-permute-start.9 = (bf16[4,256,1024]{2,1,0:T(8,128)(2,1)}, bf16[4,256,1024]{2,1,0:T(8,128)(2,1)}, u32[]{:S(2)}, u32[]{:S(2)}) collective-permute-start(bf16[4,256,1024]{2,1,0:T(8,128)(2,1)} %pad_maximum_fusion), channel_id=1, source_target_pairs={{0,16},{1,17},{2,18},{3,19},{4,20},{5,21},{6,22},{7,23},{8,24},{9,... | collective-permute-start | bytes 6291464 | tf_op jit(solution)/shard_map/ppermute | solution.py:438
  117.0 92.6 %collective-permute-start.22 = (bf16[1024,512]{1,0:T(8,128)(2,1)S(1)}, bf16[1024,512]{1,0:T(8,128)(2,1)S(1)}, u32[]{:S(2)}, u32[]{:S(2)}) collective-permute-start(bf16[1024,512]{1,0:T(8,128)(2,1)S(1)} %bitcast.170), channel_id=1, source_target_pairs={{0,16},{1,17},{2,18},{3,19},{4,20},{5,21},{6,22},{7,23},{8,24},{9,... | collective-permute-start | bytes 3145736 | tf_op jit(solution)/shard_map/ppermute | solution.py:438
  119.8 96.3 %collective-permute-start.26 = (bf16[8,64,2048]{2,1,0:T(8,128)(2,1)}, bf16[8,64,2048]{2,1,0:T(8,128)(2,1)}, u32[]{:S(2)}, u32[]{:S(2)}) collective-permute-start(bf16[8,64,2048]{2,1,0:T(8,128)(2,1)} %constant_dynamic-update-slice_fusion.13.refs_0_), channel_id=1, source_target_pairs={{0,2},{1,3},{2,0},{3,1},{4,6},{5,7},{6,4},{7,5},{8,10},{9,11},{10,... | collective-permute-start | bytes 6291464 | tf_op jit(solution)/shard_map/ppermute | solution.py:438
  159.8 61.2 %collective-permute-start.30 = (bf16[8,128,1024]{2,1,0:T(8,128)(2,1)S(1)}, bf16[8,128,1024]{2,1,0:T(8,128)(2,1)}, u32[]{:S(2)}, u32[]{:S(2)}) collective-permute-start(bf16[8,128,1024]{2,1,0:T(8,128)(2,1)S(1)} %pad_maximum_fusion.1.refs_0_), channel_id=1, source_target_pairs={{0,2},{1,3},{2,0},{3,1},{4,6},{5,7},{6,4},{7,5},{8,10},{9,11},{10,... | collective-permute-start | bytes 6291464 | tf_op jit(solution)/shard_map/ppermute | solution.py:438
  162.1 26.5 %collective-permute-start.12 = (bf16[256,128]{1,0:T(8,128)(2,1)S(1)}, bf16[256,128]{1,0:T(8,128)(2,1)S(1)}, u32[]{:S(2)}, u32[]{:S(2)}) collective-permute-start(bf16[256,128]{1,0:T(8,128)(2,1)S(1)} %get-tuple-element.43), channel_id=1, source_target_pairs={{0,2},{1,3},{2,0},{3,1},{4,6},{5,7},{6,4},{7,5},{8,18},{9,19},{10,... | collective-permute-start | bytes 196616 | tf_op jit(solution)/shard_map/ppermute | solution.py:438
  165.5 23.2 %collective-permute-start.13 = (bf16[256,128]{1,0:T(8,128)(2,1)S(1)}, bf16[256,128]{1,0:T(8,128)(2,1)S(1)}, u32[]{:S(2)}, u32[]{:S(2)}) collective-permute-start(bf16[256,128]{1,0:T(8,128)(2,1)S(1)} %get-tuple-element.44), channel_id=1, source_target_pairs={{0,6},{1,7},{2,4},{3,5},{4,2},{5,3},{6,0},{7,1},{8,22},{9,23},{10,... | collective-permute-start | bytes 196616 | tf_op jit(solution)/shard_map/ppermute | solution.py:438
  188.7 12.6 %collective-permute-start.14 = (bf16[256,128]{1,0:T(8,128)(2,1)S(1)}, bf16[256,128]{1,0:T(8,128)(2,1)S(1)}, u32[]{:S(2)}, u32[]{:S(2)}) collective-permute-start(bf16[256,128]{1,0:T(8,128)(2,1)S(1)} %get-tuple-element.45), channel_id=1, source_target_pairs={{0,8},{1,9},{2,10},{3,11},{4,12},{5,13},{6,14},{7,15},{8,24},{9,25... | collective-permute-start | bytes 196616 | tf_op jit(solution)/shard_map/ppermute | solution.py:438
  188.7 16.2 %collective-permute-start.15 = (bf16[256,128]{1,0:T(8,128)(2,1)S(1)}, bf16[256,128]{1,0:T(8,128)(2,1)S(1)}, u32[]{:S(2)}, u32[]{:S(2)}) collective-permute-start(bf16[256,128]{1,0:T(8,128)(2,1)S(1)} %get-tuple-element.46), channel_id=1, source_target_pairs={{0,10},{1,11},{2,8},{3,9},{4,14},{5,15},{6,12},{7,13},{8,26},{9,27... | collective-permute-start | bytes 196616 | tf_op jit(solution)/shard_map/ppermute | solution.py:438
  201.2 6.3 %collective-permute-start.16 = (bf16[256,128]{1,0:T(8,128)(2,1)S(1)}, bf16[256,128]{1,0:T(8,128)(2,1)S(1)}, u32[]{:S(2)}, u32[]{:S(2)}) collective-permute-start(bf16[256,128]{1,0:T(8,128)(2,1)S(1)} %get-tuple-element.47), channel_id=1, source_target_pairs={{0,12},{1,13},{2,14},{3,15},{4,8},{5,9},{6,10},{7,11},{8,28},{9,29... | collective-permute-start | bytes 196616 | tf_op jit(solution)/shard_map/ppermute | solution.py:438
  212.0 13.6 %collective-permute-start.31 = (bf16[256,1024]{1,0:T(8,128)(2,1)}, bf16[256,1024]{1,0:T(8,128)(2,1)}, u32[]{:S(2)}, u32[]{:S(2)}) collective-permute-start(bf16[256,1024]{1,0:T(8,128)(2,1)} %fusion.32), channel_id=1, source_target_pairs={{0,16},{1,17},{2,18},{3,19},{4,20},{5,21},{6,22},{7,23},{8,24},{9,... | collective-permute-start | bytes 1572872 | tf_op jit(solution)/shard_map/ppermute | solution.py:438
  229.4 5.7 %collective-permute-start.32 = (f32[256,1024]{1,0:T(8,128)S(1)}, f32[256,1024]{1,0:T(8,128)}, u32[]{:S(2)}, u32[]{:S(2)}) collective-permute-start(f32[256,1024]{1,0:T(8,128)S(1)} %fusion.72), channel_id=1, source_target_pairs={{0,16},{1,17},{2,18},{3,19},{4,20},{5,21},{6,22},{7,23},{8,24},{9,... | collective-permute-start | bytes 3145736 | tf_op jit(solution)/shard_map/ppermute | solution.py:438
  241.8 7.6 %collective-permute-start.33 = (bf16[256,1024]{1,0:T(8,128)(2,1)}, bf16[256,1024]{1,0:T(8,128)(2,1)}, u32[]{:S(2)}, u32[]{:S(2)}) collective-permute-start(bf16[256,1024]{1,0:T(8,128)(2,1)} %get-tuple-element.73), channel_id=1, source_target_pairs={{0,16},{1,17},{2,18},{3,19},{4,20},{5,21},{6,22},{7,23},{8,24},{9,... | collective-permute-start | bytes 1572872 | tf_op jit(solution)/shard_map/ppermute | solution.py:438
  254.5 10.1 %collective-permute-start.34 = (f32[256,1024]{1,0:T(8,128)S(1)}, f32[256,1024]{1,0:T(8,128)S(1)}, u32[]{:S(2)}, u32[]{:S(2)}) collective-permute-start(f32[256,1024]{1,0:T(8,128)S(1)} %fusion.84), channel_id=1, source_target_pairs={{0,16},{1,17},{2,18},{3,19},{4,20},{5,21},{6,22},{7,23},{8,24},{9,... | collective-permute-start | bytes 3145736 | tf_op jit(solution)/shard_map/ppermute | solution.py:438
  268.9 7.2 %collective-permute-start.42 = (bf16[256,128]{1,0:T(8,128)(2,1)S(1)}, bf16[256,128]{1,0:T(8,128)(2,1)S(1)}, u32[]{:S(2)}, u32[]{:S(2)}) collective-permute-start(bf16[256,128]{1,0:T(8,128)(2,1)S(1)} %get-tuple-element.93), channel_id=1, source_target_pairs={{14,0},{15,1},{12,2},{13,3},{10,4},{11,5},{8,6},{9,7},{30,8},{31,9... | collective-permute-start | bytes 196616 | tf_op jit(solution)/shard_map/ppermute | solution.py:438
  268.9 8.3 %collective-permute-start.41 = (bf16[256,128]{1,0:T(8,128)(2,1)S(1)}, bf16[256,128]{1,0:T(8,128)(2,1)S(1)}, u32[]{:S(2)}, u32[]{:S(2)}) collective-permute-start(bf16[256,128]{1,0:T(8,128)(2,1)S(1)} %get-tuple-element.94), channel_id=1, source_target_pairs={{12,0},{13,1},{14,2},{15,3},{8,4},{9,5},{10,6},{11,7},{28,8},{29,9... | collective-permute-start | bytes 196616 | tf_op jit(solution)/shard_map/ppermute | solution.py:438
  272.3 6.8 %collective-permute-start.40 = (bf16[256,128]{1,0:T(8,128)(2,1)S(1)}, bf16[256,128]{1,0:T(8,128)(2,1)S(1)}, u32[]{:S(2)}, u32[]{:S(2)}) collective-permute-start(bf16[256,128]{1,0:T(8,128)(2,1)S(1)} %get-tuple-element.95), channel_id=1, source_target_pairs={{10,0},{11,1},{8,2},{9,3},{14,4},{15,5},{12,6},{13,7},{26,8},{27,9... | collective-permute-start | bytes 196616 | tf_op jit(solution)/shard_map/ppermute | solution.py:438
  272.3 11.8 %collective-permute-start.39 = (bf16[256,128]{1,0:T(8,128)(2,1)S(1)}, bf16[256,128]{1,0:T(8,128)(2,1)S(1)}, u32[]{:S(2)}, u32[]{:S(2)}) collective-permute-start(bf16[256,128]{1,0:T(8,128)(2,1)S(1)} %get-tuple-element.96), channel_id=1, source_target_pairs={{8,0},{9,1},{10,2},{11,3},{12,4},{13,5},{14,6},{15,7},{24,8},{25,9... | collective-permute-start | bytes 196616 | tf_op jit(solution)/shard_map/ppermute | solution.py:438
  273.0 11.6 %collective-permute-start.38 = (bf16[256,128]{1,0:T(8,128)(2,1)S(1)}, bf16[256,128]{1,0:T(8,128)(2,1)S(1)}, u32[]{:S(2)}, u32[]{:S(2)}) collective-permute-start(bf16[256,128]{1,0:T(8,128)(2,1)S(1)} %get-tuple-element.97), channel_id=1, source_target_pairs={{6,0},{7,1},{4,2},{5,3},{2,4},{3,5},{0,6},{1,7},{22,8},{23,9},{20,... | collective-permute-start | bytes 196616 | tf_op jit(solution)/shard_map/ppermute | solution.py:438
  276.1 8.6 %collective-permute-start.37 = (bf16[256,128]{1,0:T(8,128)(2,1)S(1)}, bf16[256,128]{1,0:T(8,128)(2,1)S(1)}, u32[]{:S(2)}, u32[]{:S(2)}) collective-permute-start(bf16[256,128]{1,0:T(8,128)(2,1)S(1)} %get-tuple-element.98), channel_id=1, source_target_pairs={{2,0},{3,1},{0,2},{1,3},{6,4},{7,5},{4,6},{5,7},{18,8},{19,9},{16,... | collective-permute-start | bytes 196616 | tf_op jit(solution)/shard_map/ppermute | solution.py:438
  277.2 7.4 %collective-permute-start.36 = (bf16[256,128]{1,0:T(8,128)(2,1)S(1)}, bf16[256,128]{1,0:T(8,128)(2,1)S(1)}, u32[]{:S(2)}, u32[]{:S(2)}) collective-permute-start(bf16[256,128]{1,0:T(8,128)(2,1)S(1)} %get-tuple-element.99), channel_id=1, source_target_pairs={{4,0},{5,1},{6,2},{7,3},{0,4},{1,5},{2,6},{3,7},{20,8},{21,9},{22,... | collective-permute-start | bytes 196616 | tf_op jit(solution)/shard_map/ppermute | solution.py:438
  284.2 106.6 %collective-permute-start.65 = (bf16[8,128,1024]{2,1,0:T(8,128)(2,1)}, bf16[8,128,1024]{2,1,0:T(8,128)(2,1)}, u32[]{:S(2)}, u32[]{:S(2)}) collective-permute-start(bf16[8,128,1024]{2,1,0:T(8,128)(2,1)} %copy-done.4), channel_id=1, source_target_pairs={{0,2},{1,3},{2,0},{3,1},{4,6},{5,7},{6,4},{7,5},{8,10},{9,11},{10,... | collective-permute-start | bytes 6291464 | tf_op jit(solution)/shard_map/ppermute | solution.py:438
  331.0 17.9 %collective-permute-start.47 = (bf16[8,80,384]{2,1,0:T(8,128)(2,1)S(1)}, bf16[8,80,384]{2,1,0:T(8,128)(2,1)S(1)}, u32[]{:S(2)}, u32[]{:S(2)}) collective-permute-start(bf16[8,80,384]{2,1,0:T(8,128)(2,1)S(1)} %get-tuple-element.54), channel_id=1, source_target_pairs={{0,8},{1,9},{2,10},{3,11},{4,12},{5,13},{6,14},{7,15},{8,0},{9,1},... | collective-permute-start | bytes 1474568 | tf_op jit(solution)/shard_map/ppermute | solution.py:438
  348.6 47.2 %collective-permute-start.60 = (bf16[8,64,2048]{2,1,0:T(8,128)(2,1)}, bf16[8,64,2048]{2,1,0:T(8,128)(2,1)}, u32[]{:S(2)}, u32[]{:S(2)}) collective-permute-start(bf16[8,64,2048]{2,1,0:T(8,128)(2,1)} %get-tuple-element.58), channel_id=1, source_target_pairs={{0,2},{1,3},{2,0},{3,1},{4,6},{5,7},{6,4},{7,5},{8,10},{9,11},{10,... | collective-permute-start | bytes 6291464 | tf_op jit(solution)/shard_map/ppermute | solution.py:438
  349.0 9.0 %collective-permute-start.48 = (bf16[4,80,384]{2,1,0:T(8,128)(2,1)S(1)}, bf16[4,80,384]{2,1,0:T(8,128)(2,1)S(1)}, u32[]{:S(2)}, u32[]{:S(2)}) collective-permute-start(bf16[4,80,384]{2,1,0:T(8,128)(2,1)S(1)} %fusion.43), channel_id=1, source_target_pairs={{0,1},{1,0},{2,3},{3,2},{4,5},{5,4},{6,7},{7,6},{8,9},{9,8},{10,11... | collective-permute-start | bytes 737288 | tf_op jit(solution)/shard_map/ppermute | solution.py:438
  351.7 29.8 %collective-permute-start.54 = (bf16[1024,512]{1,0:T(8,128)(2,1)}, bf16[1024,512]{1,0:T(8,128)(2,1)}, u32[]{:S(2)}, u32[]{:S(2)}) collective-permute-start(bf16[1024,512]{1,0:T(8,128)(2,1)} %convolution_convert_fusion.1), channel_id=1, source_target_pairs={{0,16},{1,17},{2,18},{3,19},{4,20},{5,21},{6,22},{7,23},{8,24},{9,... | collective-permute-start | bytes 3145736 | tf_op jit(solution)/shard_map/ppermute | solution.py:438
  358.0 9.2 %collective-permute-start.51 = (bf16[80,384]{1,0:T(8,128)(2,1)S(1)}, bf16[80,384]{1,0:T(8,128)(2,1)S(1)}, u32[]{:S(2)}, u32[]{:S(2)}) collective-permute-start(bf16[80,384]{1,0:T(8,128)(2,1)S(1)} %get-tuple-element.106), channel_id=1, source_target_pairs={{0,6},{1,7},{2,4},{3,5},{4,2},{5,3},{6,0},{7,1},{8,14},{9,15},{10,... | collective-permute-start | bytes 184328 | tf_op jit(solution)/shard_map/ppermute | solution.py:438
  363.9 6.2 %collective-permute-start.50 = (bf16[80,384]{1,0:T(8,128)(2,1)S(1)}, bf16[80,384]{1,0:T(8,128)(2,1)S(1)}, u32[]{:S(2)}, u32[]{:S(2)}) collective-permute-start(bf16[80,384]{1,0:T(8,128)(2,1)S(1)} %get-tuple-element.107), channel_id=1, source_target_pairs={{0,4},{1,5},{2,6},{3,7},{4,0},{5,1},{6,2},{7,3},{8,12},{9,13},{10,... | collective-permute-start | bytes 184328 | tf_op jit(solution)/shard_map/ppermute | solution.py:438
  367.2 10.3 %collective-permute-start.49 = (bf16[80,384]{1,0:T(8,128)(2,1)S(1)}, bf16[80,384]{1,0:T(8,128)(2,1)S(1)}, u32[]{:S(2)}, u32[]{:S(2)}) collective-permute-start(bf16[80,384]{1,0:T(8,128)(2,1)S(1)} %get-tuple-element.108), channel_id=1, source_target_pairs={{0,2},{1,3},{2,0},{3,1},{4,6},{5,7},{6,4},{7,5},{8,10},{9,11},{10,... | collective-permute-start | bytes 184328 | tf_op jit(solution)/shard_map/ppermute | solution.py:438
  370.1 54.3 %collective-permute-start.43 = (bf16[4,256,1024]{2,1,0:T(8,128)(2,1)}, bf16[4,256,1024]{2,1,0:T(8,128)(2,1)}, u32[]{:S(2)}, u32[]{:S(2)}) collective-permute-start(bf16[4,256,1024]{2,1,0:T(8,128)(2,1)} %convolution_convert_fusion), channel_id=1, source_target_pairs={{0,16},{1,17},{2,18},{3,19},{4,20},{5,21},{6,22},{7,23},{8,24},{9,... | collective-permute-start | bytes 6291464 | tf_op jit(solution)/shard_map/ppermute | solution.py:438
  378.9 9.1 %collective-permute-start.53 = (f32[16,384]{1,0:T(8,128)}, f32[16,384]{1,0:T(8,128)}, u32[]{:S(2)}, u32[]{:S(2)}) collective-permute-start(f32[16,384]{1,0:T(8,128)} %slice_reduce_fusion), channel_id=1, source_target_pairs={{0,16},{1,17},{2,18},{3,19},{4,20},{5,21},{6,22},{7,23},{8,24},{9,... | collective-permute-start | bytes 73736 | tf_op jit(solution)/shard_map/ppermute | solution.py:438
  385.6 12.3 %collective-permute-start.55 = (bf16[8,64,512]{2,1,0:T(8,128)(2,1)S(1)}, bf16[8,64,512]{2,1,0:T(8,128)(2,1)}, u32[]{:S(2)}, u32[]{:S(2)}) collective-permute-start(bf16[8,64,512]{2,1,0:T(8,128)(2,1)S(1)} %get-tuple-element.56), channel_id=1, source_target_pairs={{0,2},{1,3},{2,0},{3,1},{4,6},{5,7},{6,4},{7,5},{8,10},{9,11},{10,... | collective-permute-start | bytes 1572872 | tf_op jit(solution)/shard_map/ppermute | solution.py:438
  388.0 24.7 %collective-permute-start.52 = (f32[3,64,512]{2,1,0:T(8,128)}, f32[3,64,512]{2,1,0:T(8,128)S(1)}, u32[]{:S(2)}, u32[]{:S(2)}) collective-permute-start(f32[3,64,512]{2,1,0:T(8,128)} %reshape.346), channel_id=1, source_target_pairs={{0,16},{1,17},{2,18},{3,19},{4,20},{5,21},{6,22},{7,23},{8,24},{9,... | collective-permute-start | bytes 1179656 | tf_op jit(solution)/shard_map/ppermute | solution.py:438
  394.8 24.8 %collective-permute-start.66 = (bf16[4,128,1024]{2,1,0:T(8,128)(2,1)S(1)}, bf16[4,128,1024]{2,1,0:T(8,128)(2,1)S(1)}, u32[]{:S(2)}, u32[]{:S(2)}) collective-permute-start(bf16[4,128,1024]{2,1,0:T(8,128)(2,1)S(1)} %get-tuple-element.78), channel_id=1, source_target_pairs={{0,1},{1,0},{2,3},{3,2},{4,5},{5,4},{6,7},{7,6},{8,9},{9,8},{10,11... | collective-permute-start | bytes 3145736 | tf_op jit(solution)/shard_map/ppermute | solution.py:438
  399.4 13.1 %collective-permute-start.56 = (bf16[4,64,512]{2,1,0:T(8,128)(2,1)S(1)}, bf16[4,64,512]{2,1,0:T(8,128)(2,1)S(1)}, u32[]{:S(2)}, u32[]{:S(2)}) collective-permute-start(bf16[4,64,512]{2,1,0:T(8,128)(2,1)S(1)} %get-tuple-element.86), channel_id=1, source_target_pairs={{0,1},{1,0},{2,3},{3,2},{4,5},{5,4},{6,7},{7,6},{8,9},{9,8},{10,11... | collective-permute-start | bytes 786440 | tf_op jit(solution)/shard_map/ppermute | solution.py:438
  401.7 22.0 %collective-permute-start.61 = (bf16[4,64,2048]{2,1,0:T(8,128)(2,1)S(1)}, bf16[4,64,2048]{2,1,0:T(8,128)(2,1)S(1)}, u32[]{:S(2)}, u32[]{:S(2)}) collective-permute-start(bf16[4,64,2048]{2,1,0:T(8,128)(2,1)S(1)} %get-tuple-element.80), channel_id=1, source_target_pairs={{0,1},{1,0},{2,3},{3,2},{4,5},{5,4},{6,7},{7,6},{8,9},{9,8},{10,11... | collective-permute-start | bytes 3145736 | tf_op jit(solution)/shard_map/ppermute | solution.py:438
  412.7 6.8 %collective-permute-start.57 = (bf16[2,64,512]{2,1,0:T(8,128)(2,1)S(1)}, bf16[2,64,512]{2,1,0:T(8,128)(2,1)S(1)}, u32[]{:S(2)}, u32[]{:S(2)}) collective-permute-start(bf16[2,64,512]{2,1,0:T(8,128)(2,1)S(1)} %get-tuple-element.89), channel_id=1, source_target_pairs={{0,8},{1,9},{2,10},{3,11},{4,12},{5,13},{6,14},{7,15},{8,0},{9,1},... | collective-permute-start | bytes 393224 | tf_op jit(solution)/shard_map/ppermute | solution.py:438
  419.5 8.5 %collective-permute-start.58 = (bf16[1,64,512]{2,1,0:T(8,128)(2,1)S(1)}, bf16[1,64,512]{2,1,0:T(8,128)(2,1)S(1)}, u32[]{:S(2)}, u32[]{:S(2)}) collective-permute-start(bf16[1,64,512]{2,1,0:T(8,128)(2,1)S(1)} %fusion.52), channel_id=1, source_target_pairs={{0,4},{1,5},{2,6},{3,7},{4,0},{5,1},{6,2},{7,3},{8,12},{9,13},{10,... | collective-permute-start | bytes 196616 | tf_op jit(solution)/shard_map/ppermute | solution.py:438
  420.4 38.1 %collective-permute-start.67 = (bf16[2,128,1024]{2,1,0:T(8,128)(2,1)S(1)}, bf16[2,128,1024]{2,1,0:T(8,128)(2,1)S(1)}, u32[]{:S(2)}, u32[]{:S(2)}) collective-permute-start(bf16[2,128,1024]{2,1,0:T(8,128)(2,1)S(1)} %get-tuple-element.82), channel_id=1, source_target_pairs={{0,8},{1,9},{2,10},{3,11},{4,12},{5,13},{6,14},{7,15},{8,0},{9,1},... | collective-permute-start | bytes 1572872 | tf_op jit(solution)/shard_map/ppermute | solution.py:438
  424.3 44.3 %collective-permute-start.62 = (bf16[2,64,2048]{2,1,0:T(8,128)(2,1)S(1)}, bf16[2,64,2048]{2,1,0:T(8,128)(2,1)S(1)}, u32[]{:S(2)}, u32[]{:S(2)}) collective-permute-start(bf16[2,64,2048]{2,1,0:T(8,128)(2,1)S(1)} %get-tuple-element.84), channel_id=1, source_target_pairs={{0,8},{1,9},{2,10},{3,11},{4,12},{5,13},{6,14},{7,15},{8,0},{9,1},... | collective-permute-start | bytes 1572872 | tf_op jit(solution)/shard_map/ppermute | solution.py:438
  427.4 41.5 %collective-permute-start.44 = (bf16[2,256,1024]{2,1,0:T(8,128)(2,1)S(1)}, bf16[2,256,1024]{2,1,0:T(8,128)(2,1)S(1)}, u32[]{:S(2)}, u32[]{:S(2)}) collective-permute-start(bf16[2,256,1024]{2,1,0:T(8,128)(2,1)S(1)} %slice.376), channel_id=1, source_target_pairs={{0,2},{1,3},{2,0},{3,1},{4,6},{5,7},{6,4},{7,5},{8,10},{9,11},{10,... | collective-permute-start | bytes 3145736 | tf_op jit(solution)/shard_map/ppermute | solution.py:438
  428.1 66.5 %collective-permute-start.59 = (f32[64,512]{1,0:T(8,128)S(1)}, f32[64,512]{1,0:T(8,128)S(1)}, u32[]{:S(2)}, u32[]{:S(2)}) collective-permute-start(f32[64,512]{1,0:T(8,128)S(1)} %fusion.54), channel_id=1, source_target_pairs={{0,16},{1,17},{2,18},{3,19},{4,20},{5,21},{6,22},{7,23},{8,24},{9,... | collective-permute-start | bytes 393224 | tf_op jit(solution)/shard_map/ppermute | solution.py:438
  458.7 15.5 %collective-permute-start.68 = (bf16[1,128,1024]{2,1,0:T(8,128)(2,1)S(1)}, bf16[1,128,1024]{2,1,0:T(8,128)(2,1)S(1)}, u32[]{:S(2)}, u32[]{:S(2)}) collective-permute-start(bf16[1,128,1024]{2,1,0:T(8,128)(2,1)S(1)} %fusion.37), channel_id=1, source_target_pairs={{0,4},{1,5},{2,6},{3,7},{4,0},{5,1},{6,2},{7,3},{8,12},{9,13},{10,... | collective-permute-start | bytes 786440 | tf_op jit(solution)/shard_map/ppermute | solution.py:438
  468.8 11.0 %collective-permute-start.63 = (bf16[1,64,2048]{2,1,0:T(8,128)(2,1)S(1)}, bf16[1,64,2048]{2,1,0:T(8,128)(2,1)S(1)}, u32[]{:S(2)}, u32[]{:S(2)}) collective-permute-start(bf16[1,64,2048]{2,1,0:T(8,128)(2,1)S(1)} %fusion.39), channel_id=1, source_target_pairs={{0,4},{1,5},{2,6},{3,7},{4,0},{5,1},{6,2},{7,3},{8,12},{9,13},{10,... | collective-permute-start | bytes 786440 | tf_op jit(solution)/shard_map/ppermute | solution.py:438
  469.3 16.0 %collective-permute-start.45 = (bf16[1,256,1024]{2,1,0:T(8,128)(2,1)S(1)}, bf16[1,256,1024]{2,1,0:T(8,128)(2,1)S(1)}, u32[]{:S(2)}, u32[]{:S(2)}) collective-permute-start(bf16[1,256,1024]{2,1,0:T(8,128)(2,1)S(1)} %slice.378), channel_id=1, source_target_pairs={{0,4},{1,5},{2,6},{3,7},{4,0},{5,1},{6,2},{7,3},{8,12},{9,13},{10,... | collective-permute-start | bytes 1572872 | tf_op jit(solution)/shard_map/ppermute | solution.py:438
  474.3 23.8 %collective-permute-start.69 = (f32[128,1024]{1,0:T(8,128)S(1)}, f32[128,1024]{1,0:T(8,128)}, u32[]{:S(2)}, u32[]{:S(2)}) collective-permute-start(f32[128,1024]{1,0:T(8,128)S(1)} %bitcast.190), channel_id=1, source_target_pairs={{0,16},{1,17},{2,18},{3,19},{4,20},{5,21},{6,22},{7,23},{8,24},{9,... | collective-permute-start | bytes 1572872 | tf_op jit(solution)/shard_map/ppermute | solution.py:438
  479.9 15.5 %collective-permute-start.64 = (f32[64,16,128]{2,1,0:T(8,128)S(1)}, f32[64,16,128]{2,1,0:T(8,128)S(1)}, u32[]{:S(2)}, u32[]{:S(2)}) collective-permute-start(f32[64,16,128]{2,1,0:T(8,128)S(1)} %bitcast.191), channel_id=1, source_target_pairs={{0,16},{1,17},{2,18},{3,19},{4,20},{5,21},{6,22},{7,23},{8,24},{9,... | collective-permute-start | bytes 1572872 | tf_op jit(solution)/shard_map/ppermute | solution.py:438
  486.3 14.1 %collective-permute-start.46 = (bf16[256,1024]{1,0:T(8,128)(2,1)}, bf16[256,1024]{1,0:T(8,128)(2,1)}, u32[]{:S(2)}, u32[]{:S(2)}) collective-permute-start(bf16[256,1024]{1,0:T(8,128)(2,1)} %fusion.34), channel_id=1, source_target_pairs={{0,0},{1,1},{2,2},{3,3},{4,4},{5,5},{6,6},{7,7},{8,16},{9,17},{10,... | collective-permute-start | bytes 1572872 | tf_op jit(solution)/shard_map/ppermute | solution.py:438
  (62 other events, 567.1 us)
